TPU v7x, 128 devices: a whole 4x4x4 slice. The times are simulated.
128 devices in a mesh: dp: 8 (over x_hi, z), tensor: 16 (over x_lo, y, core).
Axes of the slice: x: 4 (x_hi: 2, x_lo: 2; x = x_hi * 2 + x_lo), y: 4, z: 4, core: 2. Of those that a mesh axis runs over, the one named last changes fastest.
Arguments:
- branch_in: bfloat16 [4096, 8192], P('dp', 'tensor'), may hold values from -6 to 6
- gate_in: bfloat16 [4096, 8192], P('dp', 'tensor'), may hold values from -6 to 6
- group_proj: bfloat16 [4096, 4096], P('dp'), may hold values from -6 to 6
- step_raw: bfloat16 [4096, 128], P('dp', 'tensor'), may hold values from -4 to 27
- conv_inner: bfloat16 [4, 8192], P(None, 'tensor'), may hold values from -3 to 3
- conv_groups: bfloat16 [4, 4096], replicated, may hold values from -3 to 3
- step_bias: float32 [128], P('tensor'), may hold values from -2.5 to -1.5
- decay_log: float32 [128], P('tensor'), may hold values from -10 to 0
- skip_gain: float32 [128], P('tensor'), may hold values from 0.5 to 1.5
- norm_gain: float32 [8192], P('tensor'), may hold values from 0.5 to 1.5
- exit_mapping_matrix: bfloat16 [8192, 8192], P('tensor'), may hold values from -0.0625 to 0.0625
- cotangent: bfloat16 [4096, 8192], P(('dp', 'tensor')), may hold values from -6 to 6
Outputs:
- layer_out: bfloat16 [4096, 8192], P(('dp', 'tensor'))
- grad_branch: bfloat16 [4096, 8192], P('dp', 'tensor')
- grad_gate: bfloat16 [4096, 8192], P('dp', 'tensor')
- grad_groups: bfloat16 [4096, 4096], P('dp', 'tensor')
- grad_step: bfloat16 [4096, 128], P('dp', 'tensor')
- grad_outproj: bfloat16 [8192, 8192], P('tensor')
All inputs are finite; a program needn't handle non-finite values.
Results may differ from a plain program's by a relative error of at most 0.022.
Values may be sent and summed in bfloat16 or wider, within the bound.
A program may use at most 192 MiB of HBM per device.

v0:
```python
import jax
import jax.numpy as jnp
from jax import lax
from jax.sharding import PartitionSpec as P

HEADS = 128
HEAD_DIM = 64
STATE = 256
GROUPS = 8
KERNEL = 4
STRETCH = 128


precise = lax.Precision.HIGHEST
epsilon = 1e-05


def from_partner(x, axis, apart):
    return lax.ppermute(x, axis, [(i, i ^ 1 << apart) for i in range(lax.axis_size(axis))])


def causal_conv(signal, kernel):
    length = signal.shape[0]
    padded = jnp.pad(signal, ((KERNEL - 1, 0), (0, 0)))
    summed = kernel[0] * padded[0:length]
    for offset in range(1, KERNEL):
        summed = summed + kernel[offset] * padded[offset : offset + length]
    return summed


def widened_prefix_pass(values, step_sizes, decay_rates, inputs, readouts):
    length, head_count, head_width = values.shape
    state_width = inputs.shape[2]
    blocks = length // STRETCH
    value_blocks = values.reshape(blocks, STRETCH, head_count, head_width)
    input_blocks = inputs.reshape(blocks, STRETCH, head_count, state_width)
    readout_blocks = readouts.reshape(blocks, STRETCH, head_count, state_width)
    step_blocks = jnp.transpose(step_sizes.reshape(blocks, STRETCH, head_count), (0, 2, 1))
    log_decays = jnp.cumsum(step_blocks * decay_rates[None, :, None], axis=2)
    row_ids = lax.broadcasted_iota(jnp.int32, (STRETCH, STRETCH), 0)
    col_ids = lax.broadcasted_iota(jnp.int32, (STRETCH, STRETCH), 1)
    causal = col_ids <= row_ids
    spread = log_decays[:, :, :, None] - log_decays[:, :, None, :]
    decays = jnp.where(causal, jnp.exp(jnp.where(causal, spread, 0.0)), 0.0)
    scores = jnp.einsum("kihn,kjhn->khij", readout_blocks, input_blocks, precision=precise)
    scores = scores * decays * step_blocks[:, :, None, :]
    within = jnp.einsum("khij,kjhp->kihp", scores, value_blocks, precision=precise)
    final_logs = log_decays[:, :, -1]
    carried_state = jnp.exp(final_logs[:, :, None] - log_decays) * step_blocks
    fresh_states = jnp.einsum(
        "kjhn,khj,kjhp->khnp", input_blocks, carried_state, value_blocks, precision=precise
    )

    def advance(state_now, stretch_item):
        fade_log, fresh_state = stretch_item
        return (jnp.exp(fade_log)[:, None, None] * state_now + fresh_state, state_now)

    initial = jnp.zeros((head_count, state_width, head_width), jnp.float32)
    previous = lax.scan(advance, initial, (final_logs, fresh_states))[1]
    entering = jnp.transpose(jnp.exp(log_decays), (0, 2, 1))[:, :, :, None]
    across = jnp.einsum("kihn,khnp->kihp", readout_blocks, previous, precision=precise) * entering
    return (within + across).reshape(length, head_count, head_width)


def ssm_mixer(
    branch_in,
    gate_in,
    input_pre,
    prior_emission,
    step_raw,
    conv_inner,
    conv_input,
    conv_readout,
    step_bias,
    decay_log,
    skip_gain,
):
    length = branch_in.shape[0]
    head_count = step_raw.shape[1]
    group_count = input_pre.shape[1] // STATE
    values = jax.nn.silu(causal_conv(branch_in.astype(jnp.float32), conv_inner.astype(jnp.float32)))
    values = values.reshape(length, head_count, HEAD_DIM)
    inputs = jax.nn.silu(causal_conv(input_pre, conv_input.astype(jnp.float32))).reshape(
        length, group_count, STATE
    )
    readouts = jax.nn.silu(causal_conv(prior_emission, conv_readout.astype(jnp.float32))).reshape(
        length, group_count, STATE
    )
    inputs = jnp.repeat(inputs, head_count // group_count, axis=1)
    readouts = jnp.repeat(readouts, head_count // group_count, axis=1)
    step_sizes = jax.nn.softplus(step_raw.astype(jnp.float32) + step_bias)
    decay_rates = -jnp.exp(decay_log)
    outputs = (
        widened_prefix_pass(values, step_sizes, decay_rates, inputs, readouts)
        + skip_gain[None, :, None] * values
    )
    return outputs.reshape(length, head_count * HEAD_DIM) * jax.nn.silu(gate_in.astype(jnp.float32))


def pair_total(partial_sum):
    return partial_sum + from_partner(partial_sum, "tensor", 0)


def reduce_weights(weight_part):
    return lax.psum(weight_part.astype(jnp.bfloat16), "dp").astype(jnp.float32)


def local(
    branch_in,
    gate_in,
    group_proj,
    step_raw,
    conv_inner,
    conv_groups,
    step_bias,
    decay_log,
    skip_gain,
    norm_gain,
    exit_mapping_matrix,
    cotangent,
):
    length = branch_in.shape[0]
    head_count = step_raw.shape[1]
    group_columns = GROUPS * STATE
    group_span = HEADS * HEAD_DIM // GROUPS
    group_id = lax.axis_index("tensor") * head_count // (HEADS // GROUPS)
    input_col = group_id * STATE
    readout_col = group_columns + group_id * STATE
    input_part = lax.dynamic_slice_in_dim(group_proj, input_col, STATE, 1).astype(jnp.float32)
    readout_part = lax.dynamic_slice_in_dim(group_proj, readout_col, STATE, 1).astype(jnp.float32)
    conv_input = lax.dynamic_slice_in_dim(conv_groups, input_col, STATE, 1)
    conv_readout = lax.dynamic_slice_in_dim(conv_groups, readout_col, STATE, 1)

    def local_map(branch_part, gate_part, input_vals, readout_vals, step_part):
        return ssm_mixer(
            branch_part,
            gate_part,
            input_vals,
            readout_vals,
            step_part,
            conv_inner,
            conv_input,
            conv_readout,
            step_bias,
            decay_log,
            skip_gain,
        )

    gated_out, pullback = jax.vjp(local_map, branch_in, gate_in, input_part, readout_part, step_raw)
    inv_rms = lax.rsqrt(pair_total(jnp.sum(gated_out * gated_out, axis=1)) / group_span + epsilon)
    normed = (gated_out * inv_rms[:, None] * norm_gain).astype(jnp.bfloat16)
    layer_out = lax.psum_scatter(
        jnp.dot(normed, exit_mapping_matrix, preferred_element_type=jnp.float32).astype(
            jnp.bfloat16
        ),
        "tensor",
        scatter_dimension=0,
        tiled=True,
    )
    full_cotangent = lax.all_gather(cotangent, "tensor", axis=0, tiled=True)
    grad_normed = lax.dot_general(
        full_cotangent,
        exit_mapping_matrix,
        (((1,), (1,)), ((), ())),
        preferred_element_type=jnp.float32,
    )
    weight_part = lax.dot_general(
        normed, full_cotangent, (((0,), (0,)), ((), ())), preferred_element_type=jnp.float32
    )
    scaled = norm_gain * grad_normed
    within = pair_total(jnp.sum(gated_out * scaled, axis=1))
    grad_gated = inv_rms[:, None] * scaled - gated_out * (inv_rms**3 * within / group_span)[:, None]
    grad_branch, grad_gate, derivative_entries, grad_readouts, grad_step = pullback(grad_gated)
    padded = jnp.zeros((length, 2 * group_columns), jnp.float32)
    padded = lax.dynamic_update_slice_in_dim(padded, derivative_entries, input_col, 1)
    padded = lax.dynamic_update_slice_in_dim(padded, grad_readouts, readout_col, 1)
    grad_groups = lax.psum_scatter(
        padded.astype(jnp.bfloat16), "tensor", scatter_dimension=1, tiled=True
    )
    grad_branch, grad_gate, grad_groups, grad_step = (
        grad_branch,
        grad_gate,
        grad_groups,
        grad_step,
    )
    weight_total = reduce_weights(weight_part.astype(jnp.bfloat16).astype(jnp.float32))
    return (
        layer_out,
        grad_branch,
        grad_gate,
        grad_groups,
        grad_step,
        weight_total.astype(jnp.bfloat16),
    )


def solution(mesh):
    placed = (
        P("dp", "tensor"),
        P("dp", "tensor"),
        P("dp", None),
        P("dp", "tensor"),
        P(None, "tensor"),
        P(),
        P("tensor"),
        P("tensor"),
        P("tensor"),
        P("tensor"),
        P("tensor", None),
        P(("dp", "tensor"), None),
    )
    return jax.shard_map(
        local,
        mesh=mesh,
        in_specs=placed,
        out_specs=(
            P(("dp", "tensor"), None),
            P("dp", "tensor"),
            P("dp", "tensor"),
            P("dp", "tensor"),
            P("dp", "tensor"),
            P("tensor", None),
        ),
        check_vma=False,
    )
```

profile of v0, /device:TPU:0, one launch (start us, length us, event | category | flops | bytes accessed | tf_op | source)
XLA Modules:
  0.0 495.0 jit_solution(1128194787096292728)
XLA Ops:
  19.6 4.8 fusion.13
  24.4 8.9 %fusion.11 = f32[4,8,256,64]{3,2,1,0:T(8,128)} fusion(f32[4,128,256]{2,1,0:T(8,128)S(1)} %bitcast.149, f32[4,128,8,64]{1,0,3,2:T(4,128)S(1)} %reshape.104, f32[4,128,8]{1,2,0:T(8,128)S(1)} %get-tuple-element.392), kind=kOutput, calls=%fused_computation.27 | convolution fusion | flops 805568512 | bytes 3686400 | tf_op jit(solution)/shard_map/jvp(kjhn,khj,kjhp->khnp)/dot_general | solution.py:50
  33.3 2.5 broadcast.82.clone
  35.8 10.4 %while.36 = (s32[]{:T(128)}, f32[8,256,64]{2,1,0:T(8,128)S(1)}, f32[4,8,256,64]{3,2,1,0:T(8,128)}, f32[4,8]{1,0:T(4,128)S(1)}, f32[4,8,1,1]{1,3,2,0:T(1,128)S(1)...) while((s32[]{:T(128)}, f32[8,256,64]{2,1,0:T(8,128)S(1)}, ...), condition=%wide.region_2.3_spmd.clone, body=%wide.region_1.2_spmd.clone.sunk | while | flops 524291 | bytes 3147988 | solution.py:59
  46.2 9.0 %fusion.37 = f32[4,128,8,64]{1,3,2,0:T(8,128)S(1)} fusion(f32[4,8,256,64]{3,2,1,0:T(8,128)} %get-tuple-element.544, f32[4,128,256]{2,1,0:T(8,128)S(1)} %bitcast.153), kind=kOutput, calls=%fused_computation.51 | convolution fusion | flops 805306368 | bytes 3670016 | tf_op jit(solution)/shard_map/jvp(kihn,khnp->kihp)/dot_general | solution.py:61
  56.3 4.3 fusion.28
  60.6 2.0 copy.112
  62.6 1.9 reshape.113
  64.7 12.3 %multiply_reduce_fusion.2 = (f32[512]{0:T(512)S(1)}, f32[512]{0:T(512)S(1)}, f32[512,512]{1,0:T(8,128)}, f32[512,512]{1,0:T(8,128)}) fusion(bf16[512,512]{1,0:T(8,128)(2,1)} %param.17, f32[512,512]{1,0:T(8,128)S(1)} %reshape.113, f32[512,512]{1,0:T(8,128)S(1)} %copy-done.8, f32[512]{0:T(512)S(1)} %mul.536, ...), kind=kOutput, calls=%fused_computation.72 | convolution fusion | flops 4299422720 | bytes 21504000 | tf_op jit(solution)/shard_map/dot_general | solution.py:161
  78.4 4.0 fusion.47
  82.4 2.6 copy.82
  86.6 10.4 %fusion.16 = f32[4,8,256,64]{3,2,1,0:T(8,128)} fusion(f32[4,128,256]{2,1,0:T(8,128)} %bitcast.154, f32[4,128,8,64]{1,0,3,2:T(4,128)S(1)} %reshape.107, f32[4,128,8]{1,2,0:T(8,128)S(1)} %get-tuple-element.391), kind=kOutput, calls=%fused_computation.32 | convolution fusion | flops 805568512 | bytes 3686400 | tf_op jit(solution)/shard_map/transpose(jvp(kihn,khnp->kihp))/dot_general | solution.py:61
  97.0 5.4 %fusion.52 = f32[4,8,128,256]{3,2,1,0:T(8,128)} fusion(f32[4,8,256,64]{3,2,1,0:T(8,128)S(1)} %copy-done, f32[4,128,8,64]{1,0,3,2:T(4,128)S(1)} %reshape.107, f32[4,128,8]{1,2,0:T(8,128)S(1)} %get-tuple-element.391), kind=kOutput, calls=%fused_computation.67 | convolution fusion | flops 805568512 | bytes 7356416 | tf_op jit(solution)/shard_map/transpose(jvp(kihn,khnp->kihp))/dot_general | solution.py:61
  102.4 2.4 broadcast.82
  104.9 11.8 %while.37 = (s32[]{:T(128)}, f32[8,256,64]{2,1,0:T(8,128)S(1)}, f32[4,8]{1,0:T(4,128)S(1)}, f32[4,8,256,64]{3,2,1,0:T(8,128)}, f32[4,8,256,64]{3,2,1,0:T(8,128)}...) while((s32[]{:T(128)}, f32[8,256,64]{2,1,0:T(8,128)S(1)}, ...), condition=%wide.region_8.9_spmd.clone, body=%wide.region_6.8_spmd.clone.sunk | while | flops 786436 | bytes 3670456 | solution.py:59
  105.9 1.8 fusion.135
  116.7 6.3 %fusion.98 = (f32[4,8,128]{2,1,0:T(8,128)S(1)}, f32[4,8,128]{2,1,0:T(8,128)S(1)}, f32[4,8,128]{2,1,0:T(8,128)S(1)}, f32[4,8,128,128]{3,2,1,0:T(8,128)S(1)}) fusion(f32[4,8,128]{2,1,0:T(8,128)S(1)} %reduce_window_sum.22, f32[4,8,128,128]{3,2,1,0:T(8,128)} %fusion.13, f32[4,8,128]{2,1,0:T(8,128)S(1)} %fusion.107, pred[128,128]{1,0:T(8,128)(4,1)S(1)} %iota_compare_fusion, ...), kind=kOutput, calls=%fused_computation.157 | convolution fusion | flops 409456640 | bytes 6389760 | tf_op jit(solution)/shard_map/transpose(jvp(khij,kjhp->kihp))/dot_general | solution.py:47
  123.0 4.3 add_reduce_fusion
  129.7 4.4 fusion.72
  134.1 8.1 %fusion.4 = f32[4,128,256]{1,2,0:T(8,128)S(1)} fusion(f32[4,8,256,128]{3,2,1,0:T(8,128)S(1)} %fusion.72, f32[4,128,256]{2,1,0:T(8,128)S(1)} %bitcast.155, f32[4,8,128,128]{3,2,1,0:T(8,128)S(1)} %get-tuple-element.406, f32[4,8,128]{2,1,0:T(8,128)S(1)} %fusion.107, f32[4,8,128]{2,1,0:T(8,128)S(1)} %reduce_window_sum.22, pred[128,128]{1,0:T(8,128)(4,1)S(1)} %iota_compare_fusion), kind=kOutput, calls=%fused_computation.16 | convolution fusion | flops 1615200256 | bytes 7389184 | tf_op jit(solution)/shard_map/transpose(jvp(kihn,kjhn->khij))/dot_general | solution.py:45
  144.8 2.5 broadcast_in_dim.76
  149.2 11.6 %convolution_convert_fusion = bf16[512,8192]{1,0:T(8,128)(2,1)} fusion(bf16[512,8192]{1,0:T(8,128)(2,1)} %all-gather.2.cloned.1.call-done, f32[512,512]{1,0:T(8,128)} %get-tuple-element.367, f32[512]{0:T(512)S(1)} %copy-done.19, f32[512]{0:T(512)S(1)} %get-tuple-element.366), kind=kOutput, calls=%fused_computation.13 | convolution fusion | flops 4299948032 | bytes 17829888 | tf_op jit(solution)/shard_map/dot_general | solution.py:167
  161.1 11.7 %convolution_convert_fusion.1 = bf16[512,8192]{1,0:T(8,128)(2,1)} fusion(bf16[512,8192]{1,0:T(8,128)(2,1)} %param.26, f32[512,512]{1,0:T(8,128)} %get-tuple-element.367, f32[512]{0:T(512)S(1)} %copy-done.19, f32[512]{0:T(512)S(1)} %get-tuple-element.366), kind=kOutput, calls=%fused_computation.14 | convolution fusion | flops 4299948032 | bytes 17829888 | tf_op jit(solution)/shard_map/dot_general | solution.py:153
  172.8 10.1 %fusion.51 = (f32[4,8,128]{2,1,0:T(8,128)S(1)}, f32[4,8,64,128]{3,2,1,0:T(8,128)}) fusion(f32[4,8,128,64]{2,0,3,1:T(4,128)S(1)} %bitcast.147, f32[4,8,256,64]{3,2,1,0:T(8,128)} %get-tuple-element.209, f32[4,128,256]{2,1,0:T(8,128)S(1)} %bitcast.151), kind=kOutput, calls=%fused_computation.65 | convolution fusion | flops 805826560 | bytes 4734976 | tf_op jit(solution)/shard_map/transpose(jvp(kjhn,khj,kjhp->khnp))/dot_general | solution.py:50
  183.1 5.3 %fusion.34 = f32[4,128,8,64]{1,3,2,0:T(8,128)} fusion(f32[4,8,64,128]{3,2,1,0:T(8,128)} %get-tuple-element.408, f32[4,8,128]{2,1,0:T(8,128)S(1)} %fusion.107, f32[4,8,64,128]{3,0,2,1:T(4,128)S(1)} %bitcast.146, f32[4,8,128,128]{3,2,1,0:T(8,128)} %fusion.13, f32[4,8,128]{2,1,0:T(8,128)S(1)} %reduce_window_sum.22, pred[128,128]{1,0:T(8,128)(4,1)S(1)} %iota_compare_fusion, ...), kind=kOutput, calls=%fused_computation.50 | convolution fusion | flops 405798912 | bytes 5308416 | tf_op jit(solution)/shard_map/transpose(jvp(khij,kjhp->kihp))/dot_general | solution.py:47
  188.5 3.6 copy.113
  192.0 2.7 reshape.114
  196.2 5.0 %reduce_window_sum.23 = f32[4,8,128]{2,1,0:T(8,128)S(1)} reduce-window(f32[4,8,128]{2,1,0:T(8,128)S(1)} %fusion.106, f32[]{:T(128)} %constant.118.clone.1), window={size=1x1x128 pad=0_0x0_0x0_127}, to_apply=%region_17.18 | reduce-window | flops 520192 | bytes 32772 | tf_op jit(solution)/shard_map/transpose(jvp(jit(cumsum)))/reduce_window_sum | solution.py:39
  205.3 13.2 %reduce-scatter.5.cloned.1.call-done = bf16[512,256]{1,0:T(8,128)(2,1)} async-done(((bf16[512,4096]{1,0:T(8,128)(2,1)}), bf16[512,256]{1,0:T(8,128)(2,1)}) %reduce-scatter.5.cloned.1.call-update) | async-done | bytes 262160 | tf_op jit(solution)/shard_map/reduce_scatter | solution.py:177
  218.5 187.1 %all-reduce.18.cloned.1.call-done = bf16[512,8192]{1,0:T(8,128)(2,1)} async-done(((bf16[512,8192]{1,0:T(8,128)(2,1)}), bf16[512,8192]{1,0:T(8,128)(2,1)}) %all-reduce.18.cloned.1.call-update) | async-done | bytes 8388624 | tf_op jit(solution)/shard_map/psum | solution.py:105
  405.6 74.7 %reduce-scatter.3.cloned.1.call-done = bf16[32,8192]{1,0:T(8,128)(2,1)} async-done(((bf16[512,8192]{1,0:T(8,128)(2,1)}), bf16[32,8192]{1,0:T(8,128)(2,1)}) %reduce-scatter.3.cloned.1.call-update) | async-done | bytes 524304 | tf_op jit(solution)/shard_map/reduce_scatter | solution.py:152
  480.3 7.8 %copy.182 = bf16[512,8192]{1,0:T(8,128)(2,1)} copy(bf16[512,8192]{1,0:T(8,128)(2,1)} %all-reduce.18.cloned.1.call-done) | data formatting | bytes 16777216
  (136 shorter events, 49.5 us)
Async XLA Ops:
  7.2 57.5 %all-gather.2.cloned.1.call-start = ((), (), s32[]{:S(2)}) async-start(), calls=%async_computation.3 | async-start | bytes 8912896 | tf_op jit(solution)/shard_map/all_gather | solution.py:160
  7.9 210.6 %reduce-scatter.5.cloned.1.call-start = ((), (), s32[]{:S(2)}) async-start(), calls=%async_computation.4 | async-start | bytes 4456448 | tf_op jit(solution)/shard_map/reduce_scatter | solution.py:177
  8.0 6.5 %copy-start.22 = (f32[8]{0:T(128)S(1)}, f32[8]{0:T(128)}, u32[]{:S(2)}) copy-start(f32[8]{0:T(128)} %param.23) | copy-start | bytes 100
  8.0 6.6 %copy-start.18 = (bf16[512,8]{0,1:T(8,128)(2,1)S(1)}, bf16[512,8]{0,1:T(8,128)(2,1)}, u32[]{:S(2)}) copy-start(bf16[512,8]{0,1:T(8,128)(2,1)} %param.19) | copy-start | bytes 24580
  8.0 6.6 %copy-start.20 = (f32[8]{0:T(128)S(1)}, f32[8]{0:T(128)}, u32[]{:S(2)}) copy-start(f32[8]{0:T(128)} %param.22) | copy-start | bytes 100
  19.6 13.7 %copy-start.4 = (f32[512,256]{1,0:T(8,128)}, f32[512,256]{1,0:T(8,128)S(1)}, u32[]{:S(2)}) copy-start(f32[512,256]{1,0:T(8,128)S(1)} %get-tuple-element.372) | copy-start | bytes 1572868
  19.6 26.6 %copy-start.6 = (f32[512,256]{1,0:T(8,128)}, f32[512,256]{1,0:T(8,128)S(1)}, u32[]{:S(2)}) copy-start(f32[512,256]{1,0:T(8,128)S(1)} %get-tuple-element.409) | copy-start | bytes 1572868
  46.2 10.1 %copy-start.2 = (f32[4,8,128,128]{3,2,1,0:T(8,128)S(1)}, f32[4,8,128,128]{3,2,1,0:T(8,128)}, u32[]{:S(2)}) copy-start(f32[4,8,128,128]{3,2,1,0:T(8,128)} %fusion.13) | copy-start | bytes 6291460
  55.2 1.0 copy-start.11
  60.6 4.0 copy-start.21
  60.6 4.1 copy-start.8
  60.6 4.1 copy-start.19
  64.5 12.5 %copy-start.12 = (f32[512,512]{1,0:T(8,128)}, f32[512,512]{1,0:T(8,128)S(1)}, u32[]{:S(2)}) copy-start(f32[512,512]{1,0:T(8,128)S(1)} %reshape.113) | copy-start | bytes 3145732
  77.0 1.2 collective-permute-start
  77.0 1.3 collective-permute-start.1
  86.6 10.4 %copy-start = (f32[4,8,256,64]{3,2,1,0:T(8,128)S(1)}, f32[4,8,256,64]{3,2,1,0:T(8,128)}, u32[]{:S(2)}) copy-start(f32[4,8,256,64]{3,2,1,0:T(8,128)} %get-tuple-element.544) | copy-start | bytes 6291460
  116.6 6.4 %copy-start.3 = (f32[4,8,128,256]{3,2,1,0:T(8,128)S(1)}, f32[4,8,128,256]{3,2,1,0:T(8,128)}, u32[]{:S(2)}) copy-start(f32[4,8,128,256]{3,2,1,0:T(8,128)} %fusion.52) | copy-start | bytes 12582916
  116.7 6.4 %copy-start.5 = (f32[512,256]{1,0:T(8,128)S(1)}, f32[512,256]{1,0:T(8,128)}, u32[]{:S(2)}) copy-start(f32[512,256]{1,0:T(8,128)} %copy-done.4) | copy-start | bytes 1572868
  123.0 4.4 copy-start.16
  123.0 6.6 %copy-start.1 = (f32[4,8,256,64]{3,2,1,0:T(8,128)S(1)}, f32[4,8,256,64]{3,2,1,0:T(8,128)}, u32[]{:S(2)}) copy-start(f32[4,8,256,64]{3,2,1,0:T(8,128)} %get-tuple-element.209) | copy-start | bytes 6291460
  129.6 4.4 copy-start.7
  144.6 3.6 copy-start.13
  144.6 3.6 copy-start.14
  144.6 3.5 copy-start.15
  144.6 3.5 copy-start.17
  149.1 256.4 %all-reduce.18.cloned.1.call-start = ((), (), s32[]{:S(2)}) async-start(), calls=%async_computation.5 | async-start | bytes 16777216 | tf_op jit(solution)/shard_map/psum | solution.py:105
  160.8 319.5 %reduce-scatter.3.cloned.1.call-start = ((), (), s32[]{:S(2)}) async-start(), calls=%async_computation.2 | async-start | bytes 8912896 | tf_op jit(solution)/shard_map/reduce_scatter | solution.py:152
  188.5 12.8 %copy-start.9 = (f32[512,512]{1,0:T(8,128)S(1)}, f32[512,512]{1,0:T(8,128)}, u32[]{:S(2)}) copy-start(f32[512,512]{1,0:T(8,128)} %get-tuple-element.371) | copy-start | bytes 3145732
  188.5 12.8 %copy-start.10 = (f32[512,512]{1,0:T(8,128)S(1)}, f32[512,512]{1,0:T(8,128)}, u32[]{:S(2)}) copy-start(f32[512,512]{1,0:T(8,128)} %get-tuple-element.379) | copy-start | bytes 3145732
Sparse Core Ops, SparseCore 0:
  9.7 54.5 all-gather.1
  149.2 69.2 reduce-scatter.4
  221.0 184.4 all-reduce.17
  408.4 71.8 reduce-scatter.2
where the time goes:
time: 505 us; the launch traced here: 495 us
  waiting for transfers between devices  277 us (55%)
  matrix products  117 us (23%)
  other arithmetic  49.7 us (10%)
  local copies, waits for them, and re-layouts  36.2 us (7%)
  between operations  14.7 us (3%)
    psum x1, waiting for transfers between devices, reduce_weights(): return lax.psum(weight_part.astype(jnp.bfloat16), 'dp').astype(jnp.float32)  187 us
    reduce_scatter x1, waiting for transfers between devices, local(): lax.psum_scatter(jnp.dot(normed, exit_mapping_matrix, preferred_element_t...  74.7 us
    dot_general x3, matrix products, widened_prefix_pass(): jnp.einsum('kihn,khnp->kihp', readout_blocks, previous, precision=precise)  24.9 us
    dot_general x3, matrix products, widened_prefix_pass(): jnp.einsum('kjhn,khj,kjhp->khnp', input_blocks, carried_state, value_bloc...  23.3 us
    dot_general x3, matrix products, widened_prefix_pass(): jnp.einsum('kihn,kjhn->khij', readout_blocks, input_blocks, precision=pre...  17.2 us
    dot_general x3, matrix products, widened_prefix_pass(): jnp.einsum('khij,kjhp->kihp', scores, value_blocks, precision=precise)  15.9 us
    reduce_scatter x1, waiting for transfers between devices, local(): lax.psum_scatter(padded.astype(jnp.bfloat16), 'tensor', scatter_dimension...  13.2 us
    dot_general x1, matrix products, local(): lax.dot_general(full_cotangent, exit_mapping_matrix, (((1,), (1,)), ((),...  12.3 us
  transfers between devices with their start and end apart: 6, of which 5 were waited for; matrix products, arithmetic and copies ran while one was open for 22% of the time, Pallas kernels for 0%

commit v1 on v0

v1 whole, which is shorter than its diff:
```python
import functools
import jax
import jax.numpy as jnp
from jax import lax
from jax.experimental import pallas as pl
from jax.experimental.pallas import tpu as pltpu
from jax.sharding import PartitionSpec as P

HEADS = 128
HEAD_DIM = 64
STATE = 256
GROUPS = 8
KERNEL = 4
STRETCH = 128
LANES = 128
f32, bf16 = jnp.float32, jnp.bfloat16
epsilon = 1e-05
NN = (((1,), (0,)), ((), ()))
NT = (((1,), (1,)), ((), ()))
TN = (((0,), (0,)), ((), ()))


def mm(a, b, dims=NN):
    return lax.dot_general(a, b, dims, preferred_element_type=f32)


def mm_exact(a, b, dims=NN):
    return lax.dot_general(a, b, dims, precision=lax.Precision.HIGHEST, preferred_element_type=f32)


def iota(shape, axis):
    return lax.broadcasted_iota(jnp.int32, shape, axis)


def sigmoid(x):
    return 1.0 / (1.0 + jnp.exp(-x))


def later(x, steps):
    return jnp.where(iota(x.shape, 0) >= steps, pltpu.roll(x, steps, 0), 0.0)


def earlier(x, steps):
    length = x.shape[0]
    return jnp.where(iota(x.shape, 0) < length - steps, pltpu.roll(x, length - steps, 0), 0.0)


def conv(x, taps):
    total = taps[KERNEL - 1 : KERNEL] * x
    for steps in range(1, KERNEL):
        total = total + taps[KERNEL - 1 - steps : KERNEL - steps] * later(x, steps)
    return total


def conv_back(g, taps):
    total = taps[KERNEL - 1 : KERNEL] * g
    for steps in range(1, KERNEL):
        total = total + taps[KERNEL - 1 - steps : KERNEL - steps] * earlier(g, steps)
    return total


def silu_slope(x):
    s = sigmoid(x)
    return s * (1.0 + x * (1.0 - s))


def panels(width):
    return [slice(c, c + LANES) for c in range(0, width, LANES)]


def prepare(r):
    length, channels = r["branch"].shape
    heads = r["step"].shape[1]
    for cols in panels(channels):
        pre = conv(r["branch"][:, cols].astype(f32), r["conv_inner"][:, cols].astype(f32))
        r["v"][:, cols] = pre * sigmoid(pre)
    for source, taps, to in (("in", "conv_in", "i"), ("ro", "conv_ro", "r")):
        for cols in panels(STATE):
            pre = conv(r[source][:, cols].astype(f32), r[taps][:, cols].astype(f32))
            r[to][:, cols] = pre * sigmoid(pre)
    small = r["small"]
    small[...] = jnp.zeros_like(small)
    small[0:1, 0:heads] = r["step_bias"][...]
    small[1:2, 0:heads] = -jnp.exp(r["decay_log"][...])
    small[2:3, 0:heads] = r["skip"][...]
    r["z"][...] = jnp.zeros_like(r["z"])
    r["z"][:, 0:heads] = r["step"][...].astype(f32)
    z = r["z"][...] + small[0:1]
    r["z"][...] = z
    dt = jnp.maximum(z, 0.0) + jnp.log1p(jnp.exp(-jnp.abs(z)))
    r["dt"][...] = dt
    square = (STRETCH, STRETCH)
    below = (iota(square, 1) <= iota(square, 0)).astype(f32)
    for k in range(length // STRETCH):
        rows = slice(k * STRETCH, (k + 1) * STRETCH)
        ld = mm_exact(below, dt[rows] * small[1:2])
        r["ld"][rows] = ld
        r["ldt"][k] = jnp.transpose(ld)[0:8]


def widen(columns, pair):
    first, second = columns[:, 2 * pair : 2 * pair + 1], columns[:, 2 * pair + 1 : 2 * pair + 2]
    low = iota((1, LANES), 1) < HEAD_DIM
    return jnp.where(low, first, second)


def widen_all(row, pairs):
    return jnp.concatenate([widen(row, p) for p in range(pairs)], axis=1)


def split_pair(x):
    low = iota(x.shape, 1) < HEAD_DIM
    zero = jnp.zeros_like(x)
    return jnp.concatenate([jnp.where(low, x, zero), jnp.where(low, zero, x)], axis=0)


def decay_of(ld, ldt, head):
    square = (STRETCH, STRETCH)
    causal = iota(square, 1) <= iota(square, 0)
    spread = ld[:, head : head + 1] - ldt[head : head + 1]
    return jnp.exp(jnp.where(causal, spread, -1e30))


def ssm_forward(r):
    length, channels = r["branch"].shape
    pairs = channels // LANES
    prepare(r)
    small = r["small"]
    state = None
    for k in range(length // STRETCH):
        rows = slice(k * STRETCH, (k + 1) * STRETCH)
        i_wide, r_wide = r["i"][rows], r["r"][rows]
        i_now, r_now = i_wide.astype(bf16), r_wide.astype(bf16)
        ld, ldt, dt = r["ld"][rows], r["ldt"][k], r["dt"][rows]
        scores = mm_exact(r_wide, i_wide, NT)
        enter = jnp.exp(ld)
        last = ld[STRETCH - 1 : STRETCH]
        leave = jnp.exp(last - ld)
        held = jnp.zeros((STATE, channels), bf16) if state is None else state.astype(bf16)
        r["sprev"][k] = held
        across = None if state is None else mm(r_now, held)
        carried = []
        squares = jnp.zeros((STRETCH, 1), f32)
        for p in range(pairs):
            cols = slice(p * LANES, (p + 1) * LANES)
            value = r["v"][rows, cols]
            stepped = widen(dt, p) * value
            weights = jnp.concatenate(
                [(scores * decay_of(ld, ldt, 2 * p + h)).astype(bf16) for h in range(2)], axis=1
            )
            y = mm(weights, split_pair(stepped.astype(bf16)))
            if across is not None:
                y = y + widen(enter, p) * across[:, cols]
            y = y + widen(small[2:3], p) * value
            r["y"][rows, cols] = y
            gate = r["gate"][rows, cols].astype(f32)
            gated = y * (gate * sigmoid(gate))
            r["gated"][rows, cols] = gated
            squares = squares + jnp.sum(gated * gated, axis=1, keepdims=True)
            carried.append((widen(leave, p) * stepped).astype(bf16))
        r["squares"][rows] = squares
        fresh = mm(i_now, jnp.concatenate(carried, axis=1), TN)
        state = fresh if state is None else widen_all(jnp.exp(last), pairs) * state + fresh


def ssm_backward(r):
    length, channels = r["branch"].shape
    heads = r["step"].shape[1]
    pairs = channels // LANES
    prepare(r)
    small = r["small"]
    square = (STRETCH, STRETCH)
    row, col = iota(square, 0), iota(square, 1)
    before = (row < col).astype(bf16)
    before32 = (row < col).astype(f32)
    since32 = (row >= col).astype(f32)
    own = (iota((8, channels), 1) // HEAD_DIM == iota((8, channels), 0)).astype(bf16)
    grad_state = None
    for k in reversed(range(length // STRETCH)):
        rows = slice(k * STRETCH, (k + 1) * STRETCH)
        i_wide, r_wide = r["i"][rows], r["r"][rows]
        i_now, r_now = i_wide.astype(bf16), r_wide.astype(bf16)
        ld, ldt, dt = r["ld"][rows], r["ldt"][k], r["dt"][rows]
        scores = mm_exact(r_wide, i_wide, NT)
        enter = jnp.exp(ld)
        last = ld[STRETCH - 1 : STRETCH]
        leave = jnp.exp(last - ld)
        held = r["sprev"][k]
        across = mm(r_now, held)
        entering, leaving, crossed, direct, left = [], [], [], [], []
        grad_after = None if grad_state is None else grad_state.astype(bf16)
        from_state = None if grad_state is None else mm(i_now, grad_after)
        grad_scores = jnp.zeros(square, f32)
        straddle = []
        for p in range(pairs):
            cols = slice(p * LANES, (p + 1) * LANES)
            value = r["v"][rows, cols]
            dt_wide = widen(dt, p)
            stepped = dt_wide * value
            gate = r["gate"][rows, cols].astype(f32)
            gg = r["gg"][rows, cols]
            r["grad_gate"][rows, cols] = (gg * r["y"][rows, cols] * silu_slope(gate)).astype(bf16)
            gy = gg * (gate * sigmoid(gate))
            gys = split_pair(gy.astype(bf16))
            grad_weights = mm(gys, stepped.astype(bf16), NT)
            weights = []
            for h in range(2):
                decay = decay_of(ld, ldt, 2 * p + h)
                weight = scores * decay
                weights.append(weight.astype(bf16))
                grad_weight = grad_weights[h * STRETCH : (h + 1) * STRETCH]
                grad_scores = grad_scores + grad_weight * decay
                crossing = mm((grad_weight * weight).astype(bf16), before)
                straddle.append(
                    jnp.sum(jnp.where(row >= col, crossing, 0.0), axis=0, keepdims=True)
                )
            grad_stepped = mm(jnp.concatenate(weights, axis=0), gys, TN)
            wide_enter = widen(enter, p) * gy
            entering.append(wide_enter.astype(bf16))
            crossed.append((wide_enter * across[:, cols]).astype(bf16))
            if from_state is not None:
                wide_leave = widen(leave, p)
                back = wide_leave * from_state[:, cols]
                grad_stepped = grad_stepped + back
                left.append((back * stepped).astype(bf16))
                leaving.append((wide_leave * stepped).astype(bf16))
            direct.append((grad_stepped * value).astype(bf16))
            r["gv"][rows, cols] = dt_wide * grad_stepped + widen(small[2:3], p) * gy
        entering = jnp.concatenate(entering, axis=1)
        gs = grad_scores.astype(bf16)
        r["gr"][rows] = mm(gs, i_now) + mm(entering, held, NT)
        grad_in = mm(gs, r_now, TN)
        if grad_after is not None:
            grad_in = grad_in + mm(jnp.concatenate(leaving, axis=1), grad_after, NT)
        r["gi"][rows] = grad_in
        to_heads = lambda parts: mm(own, jnp.concatenate(parts, axis=1), NT)
        grad_x = jnp.concatenate(straddle, axis=0)
        grad_x = grad_x + mm_exact(to_heads(crossed), since32)
        if grad_state is not None:
            grad_x = grad_x + mm_exact(to_heads(left), before32)
            faded = widen_all(jnp.exp(last), pairs) * grad_state
            kept = jnp.sum(faded * held.astype(f32), axis=0, keepdims=True)
            grad_x = grad_x + jnp.sum(own.astype(f32) * kept, axis=1, keepdims=True)
        r["z8"][0:8] = grad_x
        r["z8"][8:16] = to_heads(direct)
        turned = jnp.transpose(r["z8"][...])
        grad_dt = turned[:, 8:16] + turned[:, 0:8] * small[1:2, 0:8]
        r["grad_step"][rows] = (grad_dt * sigmoid(r["z"][rows, 0:8]))[:, 0:heads].astype(bf16)
        grad_state_now = mm(r_now, entering, TN)
        grad_state = grad_state_now if grad_state is None else faded + grad_state_now
    for cols in panels(channels):
        taps = r["conv_inner"][:, cols].astype(f32)
        pre = conv(r["branch"][:, cols].astype(f32), taps)
        r["grad_branch"][:, cols] = conv_back(r["gv"][:, cols] * silu_slope(pre), taps).astype(bf16)
    for source, tap_name, grad in (("in", "conv_in", "gi"), ("ro", "conv_ro", "gr")):
        for cols in panels(STATE):
            taps = r[tap_name][:, cols].astype(f32)
            pre = conv(r[source][:, cols].astype(f32), taps)
            r[grad][:, cols] = conv_back(r[grad][:, cols] * silu_slope(pre), taps)


def shape(dims, dtype):
    return jax.ShapeDtypeStruct(dims, dtype)


NAMES = ["branch", "gate", "in", "ro", "step", "conv_inner", "conv_in", "conv_ro"]
NAMES += ["step_bias", "decay_log", "skip"]


def common_scratch(length, channels):
    return dict(
        v=pltpu.VMEM((length, channels), f32),
        i=pltpu.VMEM((length, STATE), f32),
        r=pltpu.VMEM((length, STATE), f32),
        z=pltpu.VMEM((length, LANES), f32),
        dt=pltpu.VMEM((length, LANES), f32),
        ld=pltpu.VMEM((length, LANES), f32),
        ldt=pltpu.VMEM((length // STRETCH, 8, LANES), f32),
        small=pltpu.VMEM((8, LANES), f32),
    )


def whole(dims):
    return pl.BlockSpec(dims, lambda step, group: (0,) * len(dims))


def group_block(rows, offset):
    return pl.BlockSpec((rows, STATE), lambda step, group: (0, offset + group[0]))


def call(body, group, inputs, extra, outs, scratch):
    length = inputs[0].shape[0]
    args = list(inputs) + list(extra)
    specs = []
    for index, arg in enumerate(args):
        if index in (2, 3):
            specs.append(group_block(length, GROUPS * (index - 2)))
        elif index in (6, 7):
            specs.append(group_block(KERNEL, GROUPS * (index - 6)))
        else:
            specs.append(whole(arg.shape))
    return pl.pallas_call(
        body,
        grid_spec=pltpu.PrefetchScalarGridSpec(
            num_scalar_prefetch=1,
            grid=(1,),
            in_specs=specs,
            out_specs=[whole(out.shape) for out in outs],
            scratch_shapes=scratch,
        ),
        out_shape=outs,
        compiler_params=pltpu.CompilerParams(vmem_limit_bytes=48 * 2**20),
    )(group, *args)


def forward_kernel(group, *refs):
    names = NAMES + ["y", "gated", "squares", "sprev"] + list(common_scratch(512, 512))
    ssm_forward(dict(zip(names, refs)))


def backward_kernel(group, *refs):
    names = NAMES + ["y", "sprev", "grad_normed", "inv_rms", "within", "norm_gain"]
    names += ["grad_branch", "grad_gate", "gi", "gr", "grad_step"]
    names += list(common_scratch(512, 512)) + ["gv", "z8", "gg"]
    r = dict(zip(names, refs))
    inv_rms = r["inv_rms"][...]
    shared = inv_rms * inv_rms * inv_rms * r["within"][...] * (1.0 / (HEADS * HEAD_DIM // GROUPS))
    for cols in panels(r["branch"].shape[1]):
        gate = r["gate"][:, cols].astype(f32)
        gated = r["y"][:, cols] * (gate * sigmoid(gate))
        scaled = r["norm_gain"][:, cols] * r["grad_normed"][:, cols]
        r["gg"][:, cols] = inv_rms * scaled - gated * shared
    r["z8"][...] = jnp.zeros_like(r["z8"])
    ssm_backward(r)


def swap_cores(x):
    size = lax.axis_size("tensor")
    return lax.ppermute(x, "tensor", [(i, i ^ 1) for i in range(size)])


def local(
    branch_in,
    gate_in,
    group_proj,
    step_raw,
    conv_inner,
    conv_groups,
    step_bias,
    decay_log,
    skip_gain,
    norm_gain,
    exit_mapping_matrix,
    cotangent,
):
    length, channels = branch_in.shape
    heads = step_raw.shape[1]
    group_span = HEADS * HEAD_DIM // GROUPS
    place = lax.axis_index("tensor")
    group = (place * heads // (HEADS // GROUPS)).astype(jnp.int32)[None]
    inputs = [branch_in, gate_in, group_proj, group_proj, step_raw, conv_inner, conv_groups]
    inputs += [conv_groups, step_bias[None], decay_log[None], skip_gain[None]]
    full_cotangent = lax.all_gather(cotangent, "tensor", axis=0, tiled=True)
    scratch = common_scratch(length, channels)
    y, gated_out, squares, sprev = call(
        forward_kernel,
        group,
        inputs,
        [],
        [
            shape((length, channels), f32),
            shape((length, channels), f32),
            shape((length, 1), f32),
            shape((length // STRETCH, STATE, channels), bf16),
        ],
        list(scratch.values()),
    )
    inv_rms = lax.rsqrt((squares + swap_cores(squares)) / group_span + epsilon)
    normed = (gated_out * inv_rms * norm_gain).astype(bf16)
    weight_part = lax.dot_general(normed, full_cotangent, TN, preferred_element_type=f32)
    weight_total = lax.psum(weight_part.astype(bf16), "dp")
    layer_part = jnp.dot(normed, exit_mapping_matrix, preferred_element_type=f32).astype(bf16)
    layer_out = lax.psum_scatter(layer_part, "tensor", scatter_dimension=0, tiled=True)
    grad_normed = lax.dot_general(
        full_cotangent, exit_mapping_matrix, NT, preferred_element_type=f32
    )
    within = jnp.sum(gated_out * (norm_gain * grad_normed), axis=1, keepdims=True)
    within = within + swap_cores(within)
    extra = [y, sprev, grad_normed, inv_rms, within, norm_gain[None]]
    scratch.update(
        gv=pltpu.VMEM((length, channels), f32),
        z8=pltpu.VMEM((LANES, LANES), f32),
        gg=pltpu.VMEM((length, channels), f32),
    )
    grad_branch, grad_gate, grad_in, grad_ro, grad_step = call(
        backward_kernel,
        group,
        inputs,
        extra,
        [
            shape((length, channels), bf16),
            shape((length, channels), bf16),
            shape((length, STATE), f32),
            shape((length, STATE), f32),
            shape((length, heads), bf16),
        ],
        list(scratch.values()),
    )
    odd = place % 2 == 1
    total = jnp.where(odd, grad_ro, grad_in) + swap_cores(jnp.where(odd, grad_in, grad_ro))
    size = lax.axis_size("tensor")
    moves = [(i, i // 2 + (i % 2) * (size // 2)) for i in range(size)]
    grad_groups = lax.ppermute(total.astype(bf16), "tensor", moves)
    return layer_out, grad_branch, grad_gate, grad_groups, grad_step, weight_total


def solution(mesh):
    placed = (
        P("dp", "tensor"),
        P("dp", "tensor"),
        P("dp", None),
        P("dp", "tensor"),
        P(None, "tensor"),
        P(),
        P("tensor"),
        P("tensor"),
        P("tensor"),
        P("tensor"),
        P("tensor", None),
        P(("dp", "tensor"), None),
    )
    return jax.shard_map(
        local,
        mesh=mesh,
        in_specs=placed,
        out_specs=(
            P(("dp", "tensor"), None),
            P("dp", "tensor"),
            P("dp", "tensor"),
            P("dp", "tensor"),
            P("dp", "tensor"),
            P("tensor", None),
        ),
        check_vma=False,
    )
```

time: 505 us -> 349 us (0.69)
  the two profiles are of different devices: /device:TPU:0 before, /device:TPU:11 now
where the time goes in v1:
time: 349 us; the launch traced here: 347 us
  waiting for transfers between devices  256 us (73%)
  matrix products  29.7 us (9%)
  local copies, waits for them, and re-layouts  20.6 us (6%)
  Pallas kernels  20 us (6%)
  between operations  13.9 us (4%)
  starting transfers between devices  4.68 us (1%)
    psum x1, waiting for transfers between devices, local(): weight_total = lax.psum(weight_part.astype(bf16), 'dp')  195 us
    all_gather x1, waiting for transfers between devices, local(): full_cotangent = lax.all_gather(cotangent, 'tensor', axis=0, tiled=True)  32.8 us
    pallas_call x2, Pallas kernels, call(): pl.pallas_call(body, grid_spec=pltpu.PrefetchScalarGridSpec(num_scalar_pr...  20 us
    unnamed x42, local copies, waits for them, and re-layouts  19.1 us
    reduce_scatter x1, waiting for transfers between devices, local(): lax.psum_scatter(layer_part, 'tensor', scatter_dimension=0, tiled=True)  15.7 us
    dot_general x1, matrix products, local(): lax.dot_general(full_cotangent, exit_mapping_matrix, NT, preferred_elemen...  12.6 us
    dot_general x1, matrix products, local(): lax.dot_general(normed, full_cotangent, TN, preferred_element_type=f32)  10.3 us
    ppermute x1, waiting for transfers between devices, local(): grad_groups = lax.ppermute(total.astype(bf16), 'tensor', moves)  7.66 us
  transfers between devices with their start and end apart: 7, of which 7 were waited for; matrix products, arithmetic and copies ran while one was open for 10% of the time, Pallas kernels for 6%

profile of v1, /device:TPU:11, one launch (start us, length us, event | category | flops | bytes accessed | tf_op | source)
XLA Modules:
  0.0 346.6 jit_solution(17741899530935853449)
XLA Ops:
  7.2 0.7 all-gather.2.cloned.1.call-update
  8.0 0.9 copy.23.refs_4_
  8.9 1.0 copy-done
  9.9 1.0 copy-done.2
  10.9 0.8 copy-done.6
  11.7 0.7 copy-done.10
  12.4 0.7 copy-done.12
  13.0 0.7 copy-done.14
  13.7 0.7 copy-done.16
  14.3 8.1 %shard_map.163 = (f32[512,512]{1,0:T(8,128)S(1)}, f32[512,512]{1,0:T(8,128)S(1)}, f32[512,1]{1,0:T(8,128)S(1)}, bf16[4,256,512]{2,1,0:T(8,128)(2,1)S(1)}) custom-call(s32[1]{0:T(128)} %bitcast.group, bf16[512,512]{1,0:T(8,128)(2,1)S(1)} %copy-done, bf16[512,512]{1,0:T(8,128)(2,1)S(1)} %copy-done.2, bf16[512,4096]{1,0:T(8,128)(2,1)} %refs_3_.3, ...), custom_call_target="tpu_custom_call" | custom-call | tf_op jit(solution)/shard_map/pallas_call | solution.py:302
  22.4 0.8 collective-permute-start
  23.2 1.2 collective-permute-done
  24.5 6.9 %convolution_convert_fusion.1 = bf16[512,8192]{1,0:T(8,128)(2,1)} fusion(bf16[512,8192]{1,0:T(8,128)(2,1)S(1)} %copy-done.18, f32[512,512]{1,0:T(8,128)S(1)} %get-tuple-element.15, f32[512]{0:T(512)S(1)} %copy-done.9, f32[512]{0:T(512)S(1)} %get-tuple-element.36), kind=kOutput, calls=%fused_computation.1 | convolution fusion | flops 4299948032 | bytes 17829888 | tf_op jit(solution)/shard_map/dot_general | solution.py:382
  31.6 32.8 %all-gather.2.cloned.1.call-done = bf16[512,8192]{1,0:T(8,128)(2,1)} async-done(((bf16[32,8192]{1,0:T(8,128)(2,1)}), bf16[512,8192]{1,0:T(8,128)(2,1)}) %all-gather.2.cloned.1.call-update) | async-done | bytes 8388624 | tf_op jit(solution)/shard_map/all_gather | solution.py:363
  64.4 10.3 %convolution_convert_fusion = bf16[512,8192]{1,0:T(8,128)(2,1)} fusion(bf16[512,8192]{1,0:T(8,128)(2,1)} %all-gather.2.cloned.1.call-done, f32[512,512]{1,0:T(8,128)S(1)} %get-tuple-element.15, f32[512]{0:T(512)S(1)} %copy-done.9, f32[512]{0:T(512)S(1)} %get-tuple-element.36), kind=kOutput, calls=%fused_computation | convolution fusion | flops 4299948032 | bytes 17829888 | tf_op jit(solution)/shard_map/dot_general | solution.py:380
  74.8 12.6 %multiply_reduce_fusion = (f32[512]{0:T(512)}, f32[512,512]{1,0:T(8,128)}) fusion(f32[512,512]{1,0:T(8,128)} %copy-done.5, f32[512]{0:T(512)S(1)} %copy-done.9, bf16[512,8192]{1,0:T(8,128)(2,1)} %all-gather.2.cloned.1.call-done, bf16[512,8192]{1,0:T(8,128)(2,1)} %param.22), kind=kOutput, calls=%fused_computation.2 | convolution fusion | flops 4295753216 | bytes 18878464 | tf_op jit(solution)/shard_map/dot_general | solution.py:384
  87.4 1.5 copy.26
  89.3 1.5 collective-permute-done.1
  90.8 1.1 add.27.refs_15_
  91.9 1.2 copy-done.4
  93.2 0.8 copy-done.7
  93.9 0.7 copy-done.17
  94.6 12.0 %shard_map.164 = (bf16[512,512]{1,0:T(8,128)(2,1)}, bf16[512,512]{1,0:T(8,128)(2,1)}, f32[512,256]{1,0:T(8,128)S(1)}, f32[512,256]{1,0:T(8,128)S(1)}, bf16[512,8]{1,0:T(8,128)(2,1)S(1)}) custom-call(s32[1]{0:T(128)} %bitcast.group, bf16[512,512]{1,0:T(8,128)(2,1)S(1)} %copy-done.1, bf16[512,512]{1,0:T(8,128)(2,1)S(1)} %copy-done.3, ...), custom_call_target="tpu_custom_call" | custom-call | tf_op jit(solution)/shard_map/pallas_call | solution.py:302
  106.6 0.4 collective-permute-start.2
  107.0 1.6 collective-permute-done.2
  108.8 2.8 collective-permute-start.3
  111.6 1.6 copy.29
  113.2 7.7 %collective-permute-done.3 = bf16[512,256]{1,0:T(8,128)(2,1)S(1)} collective-permute-done((bf16[512,256]{1,0:T(8,128)(2,1)S(1)}, bf16[512,256]{1,0:T(8,128)(2,1)S(1)}, u32[]{:S(2)}, u32[]{:S(2)}) %collective-permute-start.3) | collective-permute-done | bytes 262176 | tf_op jit(solution)/shard_map/ppermute | solution.py:413
  120.8 15.7 %reduce-scatter.2.cloned.1.call-done = bf16[32,8192]{1,0:T(8,128)(2,1)} async-done(((bf16[512,8192]{1,0:T(8,128)(2,1)}), bf16[32,8192]{1,0:T(8,128)(2,1)}) %reduce-scatter.2.cloned.1.call-update) | async-done | bytes 524304 | tf_op jit(solution)/shard_map/reduce_scatter | solution.py:383
  136.6 195.0 %all-reduce.2.cloned.1.call-done = bf16[512,8192]{1,0:T(8,128)(2,1)} async-done(((bf16[512,8192]{1,0:T(8,128)(2,1)}), bf16[512,8192]{1,0:T(8,128)(2,1)}) %all-reduce.2.cloned.1.call-update) | async-done | bytes 8388624 | tf_op jit(solution)/shard_map/psum | solution.py:381
  331.6 0.7 copy.33
  332.3 7.8 %copy.34 = bf16[512,8192]{1,0:T(8,128)(2,1)} copy(bf16[512,8192]{1,0:T(8,128)(2,1)} %all-reduce.2.cloned.1.call-done) | data formatting | bytes 16777216
  (37 shorter events, 1.1 us)
Async XLA Ops:
  7.2 17.3 %copy-start.9 = (f32[512]{0:T(512)S(1)}, f32[512]{0:T(512)}, u32[]{:S(2)}) copy-start(f32[512]{0:T(512)} %param.21) | copy-start | bytes 6148
  7.2 57.3 %all-gather.2.cloned.1.call-start = ((), (), s32[]{:S(2)}) async-start(), calls=%async_computation.2 | async-start | bytes 8912896 | tf_op jit(solution)/shard_map/all_gather | solution.py:363
  7.9 128.7 %reduce-scatter.2.cloned.1.call-start = ((), (), s32[]{:S(2)}) async-start(), calls=%async_computation.1 | async-start | bytes 8912896 | tf_op jit(solution)/shard_map/reduce_scatter | solution.py:383
  8.8 1.0 copy-start
  9.9 1.0 copy-start.2
  10.9 0.8 copy-start.6
  11.7 0.7 copy-start.10
  12.4 0.7 copy-start.12
  13.0 0.7 copy-start.14
  13.7 0.7 copy-start.16
  14.3 10.1 %copy-start.18 = (bf16[512,8192]{1,0:T(8,128)(2,1)S(1)}, bf16[512,8192]{1,0:T(8,128)(2,1)}, u32[]{:S(2)}) copy-start(bf16[512,8192]{1,0:T(8,128)(2,1)} %param.22) | copy-start | bytes 25165828
  22.4 42.0 %copy-start.5 = (f32[512,512]{1,0:T(8,128)}, f32[512,512]{1,0:T(8,128)S(1)}, u32[]{:S(2)}) copy-start(f32[512,512]{1,0:T(8,128)S(1)} %get-tuple-element.15) | copy-start | bytes 3145732
  22.4 1.9 collective-permute-start
  31.4 300.2 %all-reduce.2.cloned.1.call-start = ((), (), s32[]{:S(2)}) async-start(), calls=%async_computation.3 | async-start | bytes 16777216 | tf_op jit(solution)/shard_map/psum | solution.py:381
  74.7 17.1 %copy-start.1 = (bf16[512,512]{1,0:T(8,128)(2,1)S(1)}, bf16[512,512]{1,0:T(8,128)(2,1)}, u32[]{:S(2)}) copy-start(bf16[512,512]{1,0:T(8,128)(2,1)} %refs_0_.3) | copy-start | bytes 1572868
  74.7 17.1 %copy-start.3 = (bf16[512,512]{1,0:T(8,128)(2,1)S(1)}, bf16[512,512]{1,0:T(8,128)(2,1)}, u32[]{:S(2)}) copy-start(bf16[512,512]{1,0:T(8,128)(2,1)} %refs_1_.3) | copy-start | bytes 1572868
  74.8 17.1 %copy-start.11 = (bf16[4,512]{1,0:T(4,128)(2,1)S(1)}, bf16[4,512]{1,0:T(4,128)(2,1)}, u32[]{:S(2)}) copy-start(bf16[4,512]{1,0:T(4,128)(2,1)} %refs_5_.3) | copy-start | bytes 12292
  74.8 17.1 %copy-start.13 = (f32[8]{0:T(128)S(1)}, f32[8]{0:T(128)}, u32[]{:S(2)}) copy-start(f32[8]{0:T(128)} %param.18) | copy-start | bytes 100
  74.8 17.1 %copy-start.15 = (f32[8]{0:T(128)S(1)}, f32[8]{0:T(128)}, u32[]{:S(2)}) copy-start(f32[8]{0:T(128)} %param.19) | copy-start | bytes 100
  88.9 1.9 collective-permute-start.1
  91.9 1.3 copy-start.4
  93.2 0.8 copy-start.7
  93.9 0.7 copy-start.17
  106.5 2.2 copy-start.8
  106.6 2.0 collective-permute-start.2
  108.8 12.1 %collective-permute-start.3 = (bf16[512,256]{1,0:T(8,128)(2,1)S(1)}, bf16[512,256]{1,0:T(8,128)(2,1)S(1)}, u32[]{:S(2)}, u32[]{:S(2)}) collective-permute-start(bf16[512,256]{1,0:T(8,128)(2,1)S(1)} %add_convert_fusion), channel_id=1, source_target_pairs={{0,0},{1,8},{2,1},{3,9},{4,2},{5,10},{6,3},{7,11},{8,4},{9,12},{10... | collective-permute-start | bytes 786440 | tf_op jit(solution)/shard_map/ppermute | solution.py:413
Sparse Core Ops, SparseCore 0:
  9.7 54.6 all-gather.1
  67.4 69.1 reduce-scatter.1
  139.1 192.4 all-reduce.1

commit v2 on v1

v2 whole, which is shorter than its diff:
```python
import functools
from types import SimpleNamespace

import jax
import jax.numpy as jnp
from jax import lax
from jax.experimental import pallas as pl
from jax.experimental.pallas import tpu as pltpu
from jax.sharding import PartitionSpec as P

HEADS = 128
HEAD_DIM = 64
STATE = 256
GROUPS = 8
KERNEL = 4
STRETCH = 128
LANES = 128
f32, bf16 = jnp.float32, jnp.bfloat16
epsilon = 1e-05
NN = (((1,), (0,)), ((), ()))
NT = (((1,), (1,)), ((), ()))
TN = (((0,), (0,)), ((), ()))


def mm(a, b, dims=NN):
    return lax.dot_general(a, b, dims, preferred_element_type=f32)


def mm_exact(a, b, dims=NN):
    return lax.dot_general(a, b, dims, precision=lax.Precision.HIGHEST, preferred_element_type=f32)


def iota(shape, axis):
    return lax.broadcasted_iota(jnp.int32, shape, axis)


def sigmoid(x):
    return 1.0 / (1.0 + jnp.exp(-x))


def later(x, steps):
    return jnp.where(iota(x.shape, 0) >= steps, pltpu.roll(x, steps, 0), 0.0)


def earlier(x, steps):
    length = x.shape[0]
    return jnp.where(iota(x.shape, 0) < length - steps, pltpu.roll(x, length - steps, 0), 0.0)


def conv(x, taps):
    total = taps[KERNEL - 1 : KERNEL] * x
    for steps in range(1, KERNEL):
        total = total + taps[KERNEL - 1 - steps : KERNEL - steps] * later(x, steps)
    return total


def conv_back(g, taps):
    total = taps[KERNEL - 1 : KERNEL] * g
    for steps in range(1, KERNEL):
        total = total + taps[KERNEL - 1 - steps : KERNEL - steps] * earlier(g, steps)
    return total


def silu_slope(x):
    s = sigmoid(x)
    return s * (1.0 + x * (1.0 - s))


def panels(width):
    return [slice(c, c + LANES) for c in range(0, width, LANES)]


def group_taps(r, first, cols):
    start = (first + r.group) * STATE + cols.start
    return r.conv_groups[:, pl.ds(pl.multiple_of(start, LANES), LANES)].astype(f32)


def prepare(r):
    length, channels = r.branch.shape
    heads = r.step.shape[0]
    for cols in panels(channels):
        pre = conv(r.branch[:, cols].astype(f32), r.conv_inner[:, cols].astype(f32))
        r.v[:, cols] = pre * sigmoid(pre)
    for source, first, to in ((r.inp, 0, r.i), (r.ro, GROUPS, r.r)):
        for cols in panels(STATE):
            pre = conv(source[:, cols].astype(f32), group_taps(r, first, cols))
            to[:, cols] = pre * sigmoid(pre)
    small = r.small
    small[...] = jnp.zeros_like(small)
    small[0:1, 0:heads] = r.step_bias[...]
    small[1:2, 0:heads] = -jnp.exp(r.decay_log[...])
    small[2:3, 0:heads] = r.skip[...]
    r.turn[...] = jnp.zeros_like(r.turn)
    r.turn[0:8] = small[...]
    r.small_cols[...] = jnp.transpose(r.turn[...])[0:8]
    square = (STRETCH, STRETCH)
    below = (iota(square, 1) <= iota(square, 0)).astype(f32)
    for k in range(length // STRETCH):
        rows = slice(k * STRETCH, (k + 1) * STRETCH)
        r.turn[0:heads] = r.step[:, rows].astype(f32)
        z = jnp.transpose(r.turn[...]) + small[0:1]
        dt = jnp.maximum(z, 0.0) + jnp.log1p(jnp.exp(-jnp.abs(z)))
        r.dt[rows] = dt
        ld = mm_exact(below, dt * small[1:2])
        r.ld[rows] = ld
        r.ldt[k] = jnp.transpose(ld)[0:8]


def widen(columns, pair):
    first, second = columns[:, 2 * pair : 2 * pair + 1], columns[:, 2 * pair + 1 : 2 * pair + 2]
    low = iota((1, LANES), 1) < HEAD_DIM
    return jnp.where(low, first, second)


def widen_all(row, pairs):
    return jnp.concatenate([widen(row, p) for p in range(pairs)], axis=1)


def split_pair(x):
    low = iota(x.shape, 1) < HEAD_DIM
    zero = jnp.zeros_like(x)
    return jnp.concatenate([jnp.where(low, x, zero), jnp.where(low, zero, x)], axis=0)


def decay_of(ld, ldt, head):
    square = (STRETCH, STRETCH)
    causal = iota(square, 1) <= iota(square, 0)
    spread = ld[:, head : head + 1] - ldt[head : head + 1]
    return jnp.exp(jnp.where(causal, spread, -1e30))


def ssm_forward(r):
    length, channels = r.branch.shape
    pairs = channels // LANES
    prepare(r)
    small = r.small
    r.state[...] = jnp.zeros_like(r.state)

    @pl.loop(0, length // STRETCH)
    def _(k):
        rows = pl.ds(pl.multiple_of(k * STRETCH, STRETCH), STRETCH)
        i_wide, r_wide = r.i[rows], r.r[rows]
        i_now, r_now = i_wide.astype(bf16), r_wide.astype(bf16)
        ld, ldt, dt = r.ld[rows], r.ldt[k], r.dt[rows]
        scores = mm_exact(r_wide, i_wide, NT)
        enter = jnp.exp(ld)
        last = ld[STRETCH - 1 : STRETCH]
        leave = jnp.exp(last - ld)
        held = r.state[...].astype(bf16)
        r.sprev[k] = held
        across = mm(r_now, held)
        carried = []
        squares = jnp.zeros((STRETCH, LANES), f32)
        for p in range(pairs):
            cols = slice(p * LANES, (p + 1) * LANES)
            value = r.v[rows, cols]
            stepped = widen(dt, p) * value
            weights = jnp.concatenate(
                [(scores * decay_of(ld, ldt, 2 * p + h)).astype(bf16) for h in range(2)], axis=1
            )
            y = mm(weights, split_pair(stepped.astype(bf16)))
            y = y + widen(enter, p) * across[:, cols]
            y = y + widen(small[2:3], p) * value
            r.y[rows, cols] = y
            gate = r.gate[rows, cols].astype(f32)
            gated = y * (gate * sigmoid(gate))
            squares = squares + gated * gated
            carried.append((widen(leave, p) * stepped).astype(bf16))
        squares = jnp.sum(squares, axis=1, keepdims=True)
        r.squares[rows] = jnp.broadcast_to(squares, (STRETCH, LANES))
        fresh = mm(i_now, jnp.concatenate(carried, axis=1), TN)
        r.state[...] = widen_all(jnp.exp(last), pairs) * r.state[...] + fresh


def ssm_backward(r):
    length, channels = r.branch.shape
    pairs = channels // LANES
    small = r.small
    r.state[...] = jnp.zeros_like(r.state)
    square = (STRETCH, STRETCH)
    row, col = iota(square, 0), iota(square, 1)
    before = (row < col).astype(bf16)
    before32 = (row < col).astype(f32)
    since32 = (row >= col).astype(f32)
    own = (iota((8, channels), 1) // HEAD_DIM == iota((8, channels), 0)).astype(bf16)

    @pl.loop(0, length // STRETCH)
    def _(turn):
        k = length // STRETCH - 1 - turn
        rows = pl.ds(pl.multiple_of(k * STRETCH, STRETCH), STRETCH)
        i_wide, r_wide = r.i[rows], r.r[rows]
        i_now, r_now = i_wide.astype(bf16), r_wide.astype(bf16)
        ld, ldt, dt = r.ld[rows], r.ldt[k], r.dt[rows]
        scores = mm_exact(r_wide, i_wide, NT)
        enter = jnp.exp(ld)
        last = ld[STRETCH - 1 : STRETCH]
        leave = jnp.exp(last - ld)
        held = r.sprev[k]
        across = mm(r_now, held)
        entering, leaving, crossed, direct, left = [], [], [], [], []
        grad_after = r.state[...].astype(bf16)
        from_state = mm(i_now, grad_after)
        grad_scores = jnp.zeros(square, f32)
        straddle = []
        for p in range(pairs):
            cols = slice(p * LANES, (p + 1) * LANES)
            value = r.v[rows, cols]
            dt_wide = widen(dt, p)
            stepped = dt_wide * value
            gate = r.gate[rows, cols].astype(f32)
            gg = r.gg[rows, cols]
            r.grad_gate[rows, cols] = (gg * r.y[rows, cols] * silu_slope(gate)).astype(bf16)
            gy = gg * (gate * sigmoid(gate))
            gys = split_pair(gy.astype(bf16))
            grad_weights = mm(gys, stepped.astype(bf16), NT)
            weights = []
            for h in range(2):
                decay = decay_of(ld, ldt, 2 * p + h)
                weight = scores * decay
                weights.append(weight.astype(bf16))
                grad_weight = grad_weights[h * STRETCH : (h + 1) * STRETCH]
                grad_scores = grad_scores + grad_weight * decay
                crossing = mm((grad_weight * weight).astype(bf16), before)
                straddle.append(
                    jnp.sum(jnp.where(row >= col, crossing, 0.0), axis=0, keepdims=True)
                )
            grad_stepped = mm(jnp.concatenate(weights, axis=0), gys, TN)
            wide_enter = widen(enter, p) * gy
            entering.append(wide_enter.astype(bf16))
            crossed.append((wide_enter * across[:, cols]).astype(bf16))
            wide_leave = widen(leave, p)
            back = wide_leave * from_state[:, cols]
            grad_stepped = grad_stepped + back
            left.append((back * stepped).astype(bf16))
            leaving.append((wide_leave * stepped).astype(bf16))
            direct.append((grad_stepped * value).astype(bf16))
            r.gv[rows, cols] = dt_wide * grad_stepped + widen(small[2:3], p) * gy
        entering = jnp.concatenate(entering, axis=1)
        gs = grad_scores.astype(bf16)
        r.gr[rows] = mm(gs, i_now) + mm(entering, held, NT)
        grad_in = mm(gs, r_now, TN)
        grad_in = grad_in + mm(jnp.concatenate(leaving, axis=1), grad_after, NT)
        r.gi[rows] = grad_in
        to_heads = lambda parts: mm(own, jnp.concatenate(parts, axis=1), NT)
        grad_x = jnp.concatenate(straddle, axis=0)
        grad_x = grad_x + mm_exact(to_heads(crossed), since32)
        grad_x = grad_x + mm_exact(to_heads(left), before32)
        faded = widen_all(jnp.exp(last), pairs) * r.state[...]
        kept = jnp.sum(faded * held.astype(f32), axis=0, keepdims=True)
        grad_x = grad_x + jnp.sum(own.astype(f32) * kept, axis=1, keepdims=True)
        grad_dt = to_heads(direct) + grad_x * r.small_cols[:, 1:2]
        z = r.step[:, rows].astype(f32) + r.small_cols[:, 0:1]
        r.grad_step[:, rows] = (grad_dt * sigmoid(z)).astype(bf16)
        r.state[...] = faded + mm(r_now, entering, TN)

    for cols in panels(channels):
        taps = r.conv_inner[:, cols].astype(f32)
        pre = conv(r.branch[:, cols].astype(f32), taps)
        r.grad_branch[:, cols] = conv_back(r.gv[:, cols] * silu_slope(pre), taps).astype(bf16)
    for source, first, grad in ((r.inp, 0, r.gi), (r.ro, GROUPS, r.gr)):
        for cols in panels(STATE):
            taps = group_taps(r, first, cols)
            pre = conv(source[:, cols].astype(f32), taps)
            grad[:, cols] = conv_back(grad[:, cols] * silu_slope(pre), taps)


def at_rows(start, count):
    return pl.ds(pl.multiple_of(start, count), count)


class Links:
    def __init__(self, send, receive):
        self.send, self.receive, self.count = send, receive, 0

    def start(self, source, target, device):
        slot = self.count
        self.count += 1
        copy = pltpu.make_async_remote_copy(
            src_ref=source,
            dst_ref=target,
            send_sem=self.send.at[slot],
            recv_sem=self.receive.at[slot],
            device_id=device,
            device_id_type=pl.DeviceIdType.MESH,
        )
        copy.start()
        return copy


class Gather:
    def __init__(self, links, block, pair, ring, devices, own=None, core=None):
        self.links, self.block, self.pair, self.ring = links, block, pair, ring
        self.to_pair, self.up, self.down = devices
        self.core = core
        self.own = block(pair, ring, None) if own is None else own
        self.sent, self.relays = [], []

    def place(self, other, step, half=None):
        pair = lax.rem(self.pair + other, 2)
        return self.block(pair, lax.rem(self.ring + step + 4, 4), half)

    def go(self, source, target, device):
        self.sent.append(self.links.start(source, target, device))

    def relay(self, source, target):
        if self.core is not None:
            self.relays.append(self.links.start(source, target, self.core))

    def begin(self):
        here = self.place(0, 0)
        for device in (self.to_pair, self.up, self.down):
            self.go(self.own, here, device)
        self.relay(self.own, here)

    def pass_on(self, number):
        self.sent[number].wait_recv()
        if number == 0:
            piece = self.place(1, 0)
            self.go(piece, piece, self.up)
            self.go(piece, piece, self.down)
        elif number <= 4:
            other, upward = (number - 1) // 2, number % 2 == 1
            step, half = (-1, 0) if upward else (1, 1)
            piece = self.place(other, step)
            part = self.place(other, step, half)
            self.go(part, part, self.up if upward else self.down)
        else:
            other, upward = (number - 5) // 2, number % 2 == 1
            piece = self.place(other, 2, 0 if upward else 1)
        self.relay(piece, piece)

    def finish(self):
        for copy in self.relays:
            copy.wait_recv()

    def close(self):
        for copy in self.sent + self.relays:
            copy.wait_send()


COPIES = 96
LOCALS = 6


def work_scratch(length, channels, width, spread, count):
    own_rows, part = length // count, width // spread
    halfway = width // 2
    return dict(
        v=pltpu.VMEM((length, channels), f32),
        i=pltpu.VMEM((length, STATE), f32),
        r=pltpu.VMEM((length, STATE), f32),
        dt=pltpu.VMEM((length, LANES), f32),
        ld=pltpu.VMEM((length, LANES), f32),
        ldt=pltpu.VMEM((length // STRETCH, 8, LANES), f32),
        small=pltpu.VMEM((8, LANES), f32),
        state=pltpu.VMEM((STATE, channels), f32),
        sprev=pltpu.VMEM((length // STRETCH, STATE, channels), bf16),
        y=pltpu.VMEM((length, channels), f32),
        squares=pltpu.VMEM((length, LANES), f32),
        squares_there=pltpu.VMEM((length, LANES), f32),
        inv=pltpu.VMEM((length, LANES), f32),
        within=pltpu.VMEM((length, LANES), f32),
        within_there=pltpu.VMEM((length, LANES), f32),
        gv=pltpu.VMEM((length, channels), f32),
        gg=pltpu.VMEM((length, channels), f32),
        gi=pltpu.VMEM((length, STATE), f32),
        gr=pltpu.VMEM((length, STATE), f32),
        g_there=pltpu.VMEM((length, STATE), f32),
        g_sum=pltpu.VMEM((length, STATE), bf16),
        turn=pltpu.VMEM((LANES, LANES), f32),
        small_cols=pltpu.VMEM((8, LANES), f32),
        inp=pltpu.VMEM((length, STATE), bf16),
        ro=pltpu.VMEM((length, STATE), bf16),
        w=pltpu.VMEM((channels, width), bf16),
        w_there=pltpu.VMEM((channels, halfway), bf16),
        normed=pltpu.VMEM((length, channels), bf16),
        normed_there=pltpu.VMEM((length, channels), bf16),
        normed_all=pltpu.VMEM((spread, channels, length), bf16),
        cot_part=pltpu.VMEM((spread, length, part), bf16),
        cot_full=pltpu.VMEM((length, width), bf16),
        product=pltpu.VMEM((channels, part), f32),
        block=pltpu.VMEM((channels, part), bf16),
        layer_part=pltpu.VMEM((length, halfway), bf16),
        layer_there=pltpu.VMEM((count, own_rows, halfway), bf16),
        sends=pltpu.SemaphoreType.DMA((COPIES,)),
        receives=pltpu.SemaphoreType.DMA((COPIES,)),
        local_sems=pltpu.SemaphoreType.DMA((LOCALS,)),
    )


def mixer(names, spread, count, *refs):
    r = SimpleNamespace(**dict(zip(names, refs)))
    length, channels = r.branch.shape
    width = r.matrix.shape[1]
    part, halfway, own_rows = width // spread, width // 2, length // count
    group_span = HEADS * HEAD_DIM // GROUPS
    dp, place = lax.axis_index("dp"), lax.axis_index("tensor")
    core = lax.rem(place, 2)
    other_core = {"tensor": place + 1 - 2 * core}
    r.group = place // 2

    barrier = pltpu.get_barrier_semaphore()
    for k in range(1, spread):
        device = {"dp": lax.rem(dp + k, spread)}
        pl.semaphore_signal(barrier, inc=1, device_id=device, device_id_type=pl.DeviceIdType.MESH)
    for k in range(1, count):
        device = {"tensor": lax.rem(place + k, count)}
        pl.semaphore_signal(barrier, inc=1, device_id=device, device_id_type=pl.DeviceIdType.MESH)

    def bring(source, target, slot):
        copy = pltpu.make_async_copy(source, target, r.local_sems.at[slot])
        copy.start()
        return copy

    input_columns = pl.ds(pl.multiple_of(r.group * STATE, STATE), STATE)
    readout_columns = pl.ds(pl.multiple_of((GROUPS + r.group) * STATE, STATE), STATE)
    bring_in = bring(r.group_proj.at[:, input_columns], r.inp, 0)
    bring_ro = bring(r.group_proj.at[:, readout_columns], r.ro, 1)
    own_part = pl.ds(pl.multiple_of(dp * part, part), part)
    bring_part = bring(
        r.cotangent.at[:, own_part], r.cot_part.at[dp, at_rows(place * own_rows, own_rows)], 2
    )
    bring_full = bring(r.cotangent, r.cot_full.at[at_rows(place * own_rows, own_rows)], 3)
    bring_w = bring(r.matrix, r.w, 4)
    pl.semaphore_wait(barrier, spread + count - 2)

    links = Links(r.sends, r.receives)
    parts_sent = []
    for k in range(1, spread):
        to = lax.rem(dp + k, spread)
        source = r.cotangent.at[:, pl.ds(pl.multiple_of(to * part, part), part)]
        target = r.cot_part.at[dp, at_rows(place * own_rows, own_rows)]
        parts_sent.append(links.start(source, target, {"dp": to}))
    their_half = pl.ds(pl.multiple_of((1 - core) * halfway, halfway), halfway)
    w_sent = links.start(r.matrix.at[:, their_half], r.w_there, other_core)

    bring_in.wait()
    bring_ro.wait()
    ssm_forward(r)
    squares_sent = links.start(r.squares, r.squares_there, other_core)

    chip = place // 2
    column, level = chip // 4, lax.rem(chip, 4)

    def tensor_id(pair, ring):
        return (pair * 4 + ring) * 2 + core

    tensor_devices = [
        {"tensor": tensor_id(1 - column, level)},
        {"tensor": tensor_id(column, lax.rem(level + 1, 4))},
        {"tensor": tensor_id(column, lax.rem(level + 3, 4))},
    ]
    side, depth = dp // 4, lax.rem(dp, 4)
    dp_devices = [
        {"dp": (1 - side) * 4 + depth},
        {"dp": side * 4 + lax.rem(depth + 1, 4)},
        {"dp": side * 4 + lax.rem(depth + 3, 4)},
    ]

    def part_block(pair, ring, half):
        rows = at_rows(tensor_id(pair, ring) * own_rows, own_rows)
        if half is None:
            return r.cot_part.at[:, rows]
        return r.cot_part.at[half * (spread // 2) : (half + 1) * (spread // 2), rows]

    def full_block(pair, ring, half):
        rows = at_rows(tensor_id(pair, ring) * own_rows, own_rows)
        if half is None:
            return r.cot_full.at[rows]
        return r.cot_full.at[rows, half * halfway : (half + 1) * halfway]

    def normed_block(pair, ring, half):
        if half is None:
            return r.normed_all.at[pair * 4 + ring]
        rows = slice(half * (channels // 2), (half + 1) * (channels // 2))
        return r.normed_all.at[pair * 4 + ring, rows]

    def matrix_block(pair, ring, half):
        cols = pl.ds(pl.multiple_of((pair * 4 + ring) * part, part), part)
        if half is None:
            return r.grad_matrix.at[:, cols]
        rows = slice(half * (channels // 2), (half + 1) * (channels // 2))
        return r.grad_matrix.at[rows, cols]

    gather_part = Gather(links, part_block, column, level, tensor_devices, core=other_core)
    gather_full = Gather(
        links, full_block, column, level, tensor_devices, own=r.cotangent, core=other_core
    )
    gather_normed = Gather(links, normed_block, side, depth, dp_devices)
    gather_matrix = Gather(links, matrix_block, side, depth, dp_devices, own=r.block)

    bring_part.wait()
    for copy in parts_sent:
        copy.wait_recv()
    gather_part.begin()

    squares_sent.wait_recv()
    r.inv[...] = lax.rsqrt((r.squares[...] + r.squares_there[...]) / group_span + epsilon)
    for cols in panels(channels):
        gate = r.gate[:, cols].astype(f32)
        gated = r.y[:, cols] * (gate * sigmoid(gate))
        normed = gated * r.inv[...] * r.gain[:, cols]
        r.normed[:, cols] = normed.astype(bf16)
        r.normed_all[dp, cols] = jnp.transpose(normed).astype(bf16)
    gather_normed.begin()
    normed_sent = links.start(r.normed, r.normed_there, other_core)

    gather_part.pass_on(0)
    w_sent.wait_recv()
    bring_w.wait()
    normed_sent.wait_recv()
    tile = 256

    @pl.loop(0, halfway // tile)
    def _(step):
        cols = pl.ds(pl.multiple_of(step * tile, tile), tile)
        wide = pl.ds(pl.multiple_of(core * halfway + step * tile, tile), tile)
        total = mm(r.normed[...], r.w[:, wide])
        total = total + mm(r.normed_there[...], r.w_there[:, cols])
        r.layer_part[:, cols] = total.astype(bf16)

    gather_part.pass_on(1)
    gather_part.pass_on(2)
    for number in range(3):
        gather_normed.pass_on(number)
    gather_part.pass_on(3)
    gather_part.pass_on(4)
    gather_normed.pass_on(3)
    gather_normed.pass_on(4)
    gather_full.begin()
    for number in range(5, 9):
        gather_part.pass_on(number)
    gather_part.finish()

    def add_product(index, first=False):
        @pl.loop(0, part // tile)
        def _(step):
            cols = pl.ds(pl.multiple_of(step * tile, tile), tile)
            term = mm(r.normed_all[index], r.cot_part[index, :, cols])
            if first:
                r.product[:, cols] = term
            else:
                r.product[:, cols] += term

    add_product(dp, first=True)
    add_product((1 - side) * 4 + depth)
    for step in (1, 3):
        add_product(side * 4 + lax.rem(depth + step, 4))
        add_product((1 - side) * 4 + lax.rem(depth + step, 4))
    for number in range(5, 9):
        gather_normed.pass_on(number)
    add_product(side * 4 + lax.rem(depth + 2, 4))
    add_product((1 - side) * 4 + lax.rem(depth + 2, 4))
    r.block[...] = r.product[...].astype(bf16)
    gather_matrix.begin()
    bring_block = bring(r.block, matrix_block(side, depth, None), 5)

    for number in range(5):
        gather_full.pass_on(number)
    layers_sent = []
    for k in range(1, count):
        to = lax.rem(place + k, count)
        source = r.layer_part.at[at_rows(to * own_rows, own_rows)]
        layers_sent.append(links.start(source, r.layer_there.at[place], {"tensor": to}))
    for number in range(3):
        gather_matrix.pass_on(number)
    for number in range(5, 9):
        gather_full.pass_on(number)
    bring_full.wait()
    gather_full.finish()

    r.gg[...] = jnp.zeros_like(r.gg)
    deep = 512

    @pl.loop(0, width // deep)
    def _(step):
        cols = pl.ds(pl.multiple_of(step * deep, deep), deep)
        r.gg[...] += mm(r.cot_full[:, cols], r.w[:, cols], NT)

    within = jnp.zeros((length, LANES), f32)
    for cols in panels(channels):
        gate = r.gate[:, cols].astype(f32)
        gated = r.y[:, cols] * (gate * sigmoid(gate))
        scaled = r.gain[:, cols] * r.gg[:, cols]
        r.gg[:, cols] = scaled
        within = within + gated * scaled
    within = jnp.sum(within, axis=1, keepdims=True)
    r.within[...] = jnp.broadcast_to(within, (length, LANES))
    within_sent = links.start(r.within, r.within_there, other_core)
    gather_matrix.pass_on(3)
    gather_matrix.pass_on(4)
    within_sent.wait_recv()
    inv = r.inv[...]
    shared = inv * inv * inv * (r.within[...] + r.within_there[...]) * (1.0 / group_span)
    for cols in panels(channels):
        gate = r.gate[:, cols].astype(f32)
        gated = r.y[:, cols] * (gate * sigmoid(gate))
        r.gg[:, cols] = inv * r.gg[:, cols] - gated * shared
    ssm_backward(r)

    given = links.count
    links.count += 1

    def give(source):
        return pltpu.make_async_remote_copy(
            src_ref=source,
            dst_ref=r.g_there,
            send_sem=links.send.at[given],
            recv_sem=links.receive.at[given],
            device_id=other_core,
            device_id_type=pl.DeviceIdType.MESH,
        )

    @pl.when(core == 0)
    def _():
        give(r.gr).start()

    @pl.when(core == 1)
    def _():
        give(r.gi).start()

    for number in range(5, 9):
        gather_matrix.pass_on(number)
    r.layer_there[place] = r.layer_part[at_rows(place * own_rows, own_rows)]
    for copy in layers_sent:
        copy.wait_recv()
    for half in range(2):
        total = r.layer_there[half].astype(f32)
        for source in range(half + 2, count, 2):
            total = total + r.layer_there[source].astype(f32)
        r.layer_out[:, half * halfway : (half + 1) * halfway] = total.astype(bf16)

    give(r.gr).wait()

    @pl.when(core == 0)
    def _():
        r.g_sum[...] = (r.gi[...] + r.g_there[...]).astype(bf16)

    @pl.when(core == 1)
    def _():
        r.g_sum[...] = (r.gr[...] + r.g_there[...]).astype(bf16)

    owner = chip + core * (count // 2)

    @pl.when(owner == place)
    def _():
        r.grad_groups[...] = r.g_sum[...]

    @pl.when(owner != place)
    def _():
        links.start(r.g_sum, r.grad_groups, {"tensor": owner}).wait()

    bring_block.wait()
    for copy in parts_sent + layers_sent + [w_sent, squares_sent, normed_sent, within_sent]:
        copy.wait_send()
    for gather in (gather_part, gather_full, gather_normed, gather_matrix):
        gather.close()


def shape(dims, dtype):
    return jax.ShapeDtypeStruct(dims, dtype)


def hand_over(arrays):
    number = len(arrays)

    def body(*refs):
        sems = refs[2 * number]
        copies = [
            pltpu.make_async_copy(refs[k], refs[number + k], sems.at[k]) for k in range(number)
        ]
        for copy in copies:
            copy.start()
        for copy in copies:
            copy.wait()

    return pl.pallas_call(
        body,
        out_shape=[shape(array.shape, array.dtype) for array in arrays],
        in_specs=[pl.BlockSpec(memory_space=pltpu.HBM)] * number,
        out_specs=[pl.BlockSpec(memory_space=pltpu.HBM)] * number,
        scratch_shapes=[pltpu.SemaphoreType.DMA((number,))],
    )(*arrays)


def local(
    spread,
    count,
    branch_in,
    gate_in,
    group_proj,
    step_raw,
    conv_inner,
    conv_groups,
    step_bias,
    decay_log,
    skip_gain,
    norm_gain,
    exit_mapping_matrix,
    cotangent,
):
    length, channels = branch_in.shape
    heads = step_raw.shape[1]
    width = exit_mapping_matrix.shape[1]
    operands = dict(
        branch=branch_in,
        gate=gate_in,
        step=step_raw.T,
        conv_inner=conv_inner,
        conv_groups=conv_groups,
        step_bias=step_bias[None],
        decay_log=decay_log[None],
        skip=skip_gain[None],
        gain=norm_gain[None],
        group_proj=group_proj,
        matrix=exit_mapping_matrix,
        cotangent=cotangent,
    )
    results = dict(
        layer_out=shape((length // count, width), bf16),
        grad_branch=shape((length, channels), bf16),
        grad_gate=shape((length, channels), bf16),
        grad_groups=shape((length, STATE), bf16),
        grad_step=shape((heads, length), bf16),
        grad_matrix=shape((channels, width), bf16),
    )
    scratch = work_scratch(length, channels, width, spread, count)
    far = ("group_proj", "matrix", "cotangent", "grad_matrix")

    def spec(name):
        return pl.BlockSpec(memory_space=pl.ANY if name in far else pltpu.VMEM)

    names = list(operands) + list(results) + list(scratch)
    made = pl.pallas_call(
        functools.partial(mixer, names, spread, count),
        out_shape=list(results.values()),
        in_specs=[spec(name) for name in operands],
        out_specs=[spec(name) for name in results],
        scratch_shapes=list(scratch.values()),
        compiler_params=pltpu.CompilerParams(
            collective_id=0, has_side_effects=True, vmem_limit_bytes=62 * 2**20
        ),
    )(*operands.values())
    made = hand_over(made)
    turned = ("grad_step",)
    return tuple(array.T if name in turned else array for name, array in zip(results, made))


def solution(mesh):
    placed = (
        P("dp", "tensor"),
        P("dp", "tensor"),
        P("dp", None),
        P("dp", "tensor"),
        P(None, "tensor"),
        P(),
        P("tensor"),
        P("tensor"),
        P("tensor"),
        P("tensor"),
        P("tensor", None),
        P(("dp", "tensor"), None),
    )
    return jax.shard_map(
        functools.partial(local, mesh.shape["dp"], mesh.shape["tensor"]),
        mesh=mesh,
        in_specs=placed,
        out_specs=(
            P(("dp", "tensor"), None),
            P("dp", "tensor"),
            P("dp", "tensor"),
            P("dp", "tensor"),
            P("dp", "tensor"),
            P("tensor", None),
        ),
        check_vma=False,
    )
```

time: 349 us -> 476 us (1.36)
  Pallas kernels: 20 us -> 472 us
  waiting for transfers between devices: 256 us -> 0 us
  matrix products: 29.7 us -> 0 us
  local copies, waits for them, and re-layouts: 20.6 us -> 0 us
  between operations: 13.9 us -> 0.81 us
    pallas_call x2, Pallas kernels: 20 us -> 472 us  [the longest x1 311 us: hand_over(): pl.pallas_call(body, out_shape=[shape(array.shape, array.dtype) for array...]
    psum x1 -> x0, waiting for transfers between devices: 195 us -> none  [local(): weight_total = lax.psum(weight_part.astype(bf16), 'dp')]
    all_gather x1 -> x0, waiting for transfers between devices: 32.8 us -> none  [local(): full_cotangent = lax.all_gather(cotangent, 'tensor', axis=0, tiled=True)]
    dot_general x3 -> x0, matrix products: 29.7 us -> none  [the longest x1 12.6 us: local(): lax.dot_general(full_cotangent, exit_mapping_matrix, NT, preferred_elemen...]
    unnamed x42 -> x0, local copies, waits for them, and re-layouts: 19.1 us -> none
    reduce_scatter x1 -> x0, waiting for transfers between devices: 15.7 us -> none  [local(): lax.psum_scatter(layer_part, 'tensor', scatter_dimension=0, tiled=True)]
    ppermute x4 -> x0, waiting for transfers between devices: 11.9 us -> none  [the longest x1 7.66 us: local(): grad_groups = lax.ppermute(total.astype(bf16), 'tensor', moves)]
  transfers between devices with their start and end apart: 7 -> 0, of which waited for: 7 -> 0; matrix products, arithmetic and copies ran while one was open for 10% -> 0% of each run, Pallas kernels for 6% -> 0%
where the time goes in v2:
time: 476 us; the launch traced here: 473 us
  Pallas kernels  472 us (99%)
    pallas_call x1, Pallas kernels, hand_over(): pl.pallas_call(body, out_shape=[shape(array.shape, array.dtype) for array...  311 us
    pallas_call x1, Pallas kernels, local(): pl.pallas_call(functools.partial(mixer, names, spread, count), out_shape=...  161 us

profile of v2, /device:TPU:11, one launch (start us, length us, event | category | flops | bytes accessed | tf_op | source)
XLA Modules:
  0.0 473.1 jit_solution(16276834595328555478)
XLA Ops:
  0.6 161.2 %shard_map.163 = (bf16[32,8192]{1,0:T(8,128)(2,1)}, bf16[512,512]{1,0:T(8,128)(2,1)}, bf16[512,512]{1,0:T(8,128)(2,1)}, bf16[512,256]{1,0:T(8,128)(2,1)}, bf16[8...) custom-call(bf16[512,512]{1,0:T(8,128)(2,1)} %refs_0_.1, bf16[512,512]{1,0:T(8,128)(2,1)} %refs_1_.1, bf16[8,512]{1,0:T(8,128)(2,1)} %bitcast.6, ...), custom_call_target="tpu_custom_call" | custom-call | tf_op jit(solution)/shard_map/pallas_call | solution.py:734
  161.8 311.1 %shard_map.164 = (bf16[32,8192]{1,0:T(8,128)(2,1)}, bf16[512,512]{1,0:T(8,128)(2,1)}, bf16[512,512]{1,0:T(8,128)(2,1)}, bf16[512,256]{1,0:T(8,128)(2,1)}, bf16[8...) custom-call(bf16[32,8192]{1,0:T(8,128)(2,1)} %get-tuple-element.18.refs_0_, bf16[512,512]{1,0:T(8,128)(2,1)} %get-tuple-element.19.refs_1_, ...), custom_call_target="tpu_custom_call" | custom-call | tf_op jit(solution)/shard_map/pallas_call | solution.py:677

commit v3 on v2

--- a/solution.py
+++ b/solution.py
@@ -288,10 +288,10 @@
 
 
 class Gather:
-    def __init__(self, links, block, pair, ring, devices, own=None, core=None):
+    def __init__(self, links, block, pair, ring, devices, own=None, core=None, store=None):
         self.links, self.block, self.pair, self.ring = links, block, pair, ring
         self.to_pair, self.up, self.down = devices
-        self.core = core
+        self.core, self.store = core, store
         self.own = block(pair, ring, None) if own is None else own
         self.sent, self.relays = [], []
 
@@ -328,6 +328,17 @@
             other, upward = (number - 5) // 2, number % 2 == 1
             piece = self.place(other, 2, 0 if upward else 1)
         self.relay(piece, piece)
+        if self.store is not None:
+            self.store(*self.arrived(number))
+
+    def arrived(self, number):
+        other, upward = (0, True) if number == 0 else ((number - 1) % 4 // 2, number % 2 == 1)
+        if number == 0:
+            return 1 - self.pair, self.ring
+        step = 2 if number > 4 else (-1 if upward else 1)
+        pair = lax.rem(self.pair + other, 2)
+        half = None if number < 5 else (0 if upward else 1)
+        return pair, lax.rem(self.ring + step + 4, 4), half
 
     def finish(self):
         for copy in self.relays:
@@ -339,7 +350,7 @@
 
 
 COPIES = 96
-LOCALS = 6
+LOCALS = 15
 
 
 def work_scratch(length, channels, width, spread, count):
@@ -384,6 +395,7 @@
         layer_there=pltpu.VMEM((count, own_rows, halfway), bf16),
         sends=pltpu.SemaphoreType.DMA((COPIES,)),
         receives=pltpu.SemaphoreType.DMA((COPIES,)),
+        ready=pltpu.SemaphoreType.REGULAR,
         local_sems=pltpu.SemaphoreType.DMA((LOCALS,)),
     )
 
@@ -476,18 +488,28 @@
         return r.normed_all.at[pair * 4 + ring, rows]
 
     def matrix_block(pair, ring, half):
+        index = pair * 4 + ring
+        if half is None:
+            return r.cot_part.at[index]
+        return r.cot_part.at[index, half * (channels // 2) : (half + 1) * (channels // 2)]
+
+    stored = []
+
+    def store(pair, ring, half=None):
         cols = pl.ds(pl.multiple_of((pair * 4 + ring) * part, part), part)
-        if half is None:
-            return r.grad_matrix.at[:, cols]
-        rows = slice(half * (channels // 2), (half + 1) * (channels // 2))
-        return r.grad_matrix.at[rows, cols]
+        target = r.grad_matrix.at[:, cols]
+        if half is not None:
+            target = r.grad_matrix.at[half * (channels // 2) : (half + 1) * (channels // 2), cols]
+        stored.append(bring(matrix_block(pair, ring, half), target, 5 + len(stored)))
 
     gather_part = Gather(links, part_block, column, level, tensor_devices, core=other_core)
     gather_full = Gather(
         links, full_block, column, level, tensor_devices, own=r.cotangent, core=other_core
     )
     gather_normed = Gather(links, normed_block, side, depth, dp_devices)
-    gather_matrix = Gather(links, matrix_block, side, depth, dp_devices, own=r.block)
+    gather_matrix = Gather(
+        links, matrix_block, side, depth, dp_devices, own=r.block, store=store
+    )
 
     bring_part.wait()
     for copy in parts_sent:
@@ -552,8 +574,13 @@
     add_product(side * 4 + lax.rem(depth + 2, 4))
     add_product((1 - side) * 4 + lax.rem(depth + 2, 4))
     r.block[...] = r.product[...].astype(bf16)
+    gather_part.close()
+    for device in dp_devices:
+        pl.semaphore_signal(r.ready, inc=1, device_id=device, device_id_type=pl.DeviceIdType.MESH)
+    pl.semaphore_wait(r.ready, len(dp_devices))
     gather_matrix.begin()
-    bring_block = bring(r.block, matrix_block(side, depth, None), 5)
+    own_columns = pl.ds(pl.multiple_of(dp * part, part), part)
+    bring_block = bring(r.block, r.grad_matrix.at[:, own_columns], 5 + 9)
 
     for number in range(5):
         gather_full.pass_on(number)
@@ -650,10 +677,11 @@
     def _():
         links.start(r.g_sum, r.grad_groups, {"tensor": owner}).wait()
 
-    bring_block.wait()
+    for copy in stored + [bring_block]:
+        copy.wait()
     for copy in parts_sent + layers_sent + [w_sent, squares_sent, normed_sent, within_sent]:
         copy.wait_send()
-    for gather in (gather_part, gather_full, gather_normed, gather_matrix):
+    for gather in (gather_full, gather_normed, gather_matrix):
         gather.close()
 
 
@@ -662,24 +690,39 @@
 
 
 def hand_over(arrays):
-    number = len(arrays)
+    number, most = len(arrays), 512 * 2**10
+    pieces = []
+    for k, array in enumerate(arrays):
+        rows, cols = array.shape
+        count = max(1, 2 * rows * cols // most)
+        height = rows // count
+        pieces += [(k, slice(n * height, (n + 1) * height)) for n in range(count)]
 
     def body(*refs):
-        sems = refs[2 * number]
-        copies = [
-            pltpu.make_async_copy(refs[k], refs[number + k], sems.at[k]) for k in range(number)
-        ]
-        for copy in copies:
+        sources, targets = refs[:number], refs[number : 2 * number]
+        held, arrive, leave = refs[2 * number : 3 * number], refs[-2], refs[-1]
+        coming, going = [], []
+        for n, (k, rows) in enumerate(pieces):
+            copy = pltpu.make_async_copy(sources[k].at[rows], held[k].at[rows], arrive.at[n])
             copy.start()
-        for copy in copies:
+            coming.append(copy)
+        for n, (k, rows) in enumerate(pieces):
+            coming[n].wait()
+            copy = pltpu.make_async_copy(held[k].at[rows], targets[k].at[rows], leave.at[n])
+            copy.start()
+            going.append(copy)
+        for copy in going:
             copy.wait()
 
+    scratch = [pltpu.VMEM(array.shape, array.dtype) for array in arrays]
+    scratch += [pltpu.SemaphoreType.DMA((len(pieces),))] * 2
     return pl.pallas_call(
         body,
         out_shape=[shape(array.shape, array.dtype) for array in arrays],
         in_specs=[pl.BlockSpec(memory_space=pltpu.HBM)] * number,
         out_specs=[pl.BlockSpec(memory_space=pltpu.HBM)] * number,
-        scratch_shapes=[pltpu.SemaphoreType.DMA((number,))],
+        scratch_shapes=scratch,
+        compiler_params=pltpu.CompilerParams(vmem_limit_bytes=62 * 2**20),
     )(*arrays)
 
 

time: 476 us -> 175 us (0.37)
  Pallas kernels: 472 us -> 175 us
    pallas_call x1, Pallas kernels: 311 us -> 7.92 us  [hand_over(): pl.pallas_call(body, out_shape=[shape(array.shape, array.dtype) for array...]
    pallas_call x1, Pallas kernels: 161 us -> 167 us  [local(): pl.pallas_call(functools.partial(mixer, names, spread, count), out_shape=...]
where the time goes in v3:
time: 175 us
  Pallas kernels  175 us (100%)
    pallas_call x1, Pallas kernels, local(): pl.pallas_call(functools.partial(mixer, names, spread, count), out_shape=...  167 us
    pallas_call x1, Pallas kernels, hand_over(): pl.pallas_call(body, out_shape=[shape(array.shape, array.dtype) for array...  7.92 us

profile of v3, /device:TPU:11, one launch (start us, length us, event | category | flops | bytes accessed | tf_op | source)
XLA Modules:
  0.0 175.3 jit_solution(14066068664282245074)
XLA Ops:
  0.6 166.6 %shard_map.163 = (bf16[32,8192]{1,0:T(8,128)(2,1)}, bf16[512,512]{1,0:T(8,128)(2,1)}, bf16[512,512]{1,0:T(8,128)(2,1)}, bf16[512,256]{1,0:T(8,128)(2,1)}, bf16[8...) custom-call(bf16[512,512]{1,0:T(8,128)(2,1)} %refs_0_.1, bf16[512,512]{1,0:T(8,128)(2,1)} %refs_1_.1, bf16[8,512]{1,0:T(8,128)(2,1)} %bitcast.6, ...), custom_call_target="tpu_custom_call" | custom-call | tf_op jit(solution)/shard_map/pallas_call | solution.py:777
  167.3 7.9 %shard_map.164 = (bf16[32,8192]{1,0:T(8,128)(2,1)}, bf16[512,512]{1,0:T(8,128)(2,1)}, bf16[512,512]{1,0:T(8,128)(2,1)}, bf16[512,256]{1,0:T(8,128)(2,1)}, bf16[8...) custom-call(bf16[32,8192]{1,0:T(8,128)(2,1)} %get-tuple-element.18.refs_0_, bf16[512,512]{1,0:T(8,128)(2,1)} %get-tuple-element.19.refs_1_, ...), custom_call_target="tpu_custom_call" | custom-call | tf_op jit(solution)/shard_map/pallas_call | solution.py:719

commit v4 on v3

--- a/solution.py
+++ b/solution.py
@@ -585,12 +585,20 @@
     for number in range(5):
         gather_full.pass_on(number)
     layers_sent = []
-    for k in range(1, count):
-        to = lax.rem(place + k, count)
-        source = r.layer_part.at[at_rows(to * own_rows, own_rows)]
-        layers_sent.append(links.start(source, r.layer_there.at[place], {"tensor": to}))
-    for number in range(3):
-        gather_matrix.pass_on(number)
+    column_size = count // 2
+    in_column = lax.rem(place, column_size)
+
+    def send_layers(to_column, first):
+        for k in range(first, column_size):
+            to = to_column * column_size + lax.rem(in_column + k, column_size)
+            source = r.layer_part.at[at_rows(to * own_rows, own_rows)]
+            layers_sent.append(links.start(source, r.layer_there.at[place], {"tensor": to}))
+
+    send_layers(column, 1)
+    gather_matrix.pass_on(0)
+    send_layers(1 - column, 0)
+    gather_matrix.pass_on(1)
+    gather_matrix.pass_on(2)
     for number in range(5, 9):
         gather_full.pass_on(number)
     bring_full.wait()

time: 175 us -> 163 us (0.931)
  Pallas kernels: 175 us -> 161 us
    pallas_call x1, Pallas kernels: 167 us -> 153 us  [local(): pl.pallas_call(functools.partial(mixer, names, spread, count), out_shape=...]
where the time goes in v4:
time: 163 us; the launch traced here: 162 us
  Pallas kernels  161 us (99%)
    pallas_call x1, Pallas kernels, local(): pl.pallas_call(functools.partial(mixer, names, spread, count), out_shape=...  153 us
    pallas_call x1, Pallas kernels, hand_over(): pl.pallas_call(body, out_shape=[shape(array.shape, array.dtype) for array...  7.92 us

profile of v4, /device:TPU:11, one launch (start us, length us, event | category | flops | bytes accessed | tf_op | source)
XLA Modules:
  0.0 161.8 jit_solution(2768756141493893108)
XLA Ops:
  0.6 153.1 %shard_map.163 = (bf16[32,8192]{1,0:T(8,128)(2,1)}, bf16[512,512]{1,0:T(8,128)(2,1)}, bf16[512,512]{1,0:T(8,128)(2,1)}, bf16[512,256]{1,0:T(8,128)(2,1)}, bf16[8...) custom-call(bf16[512,512]{1,0:T(8,128)(2,1)} %refs_0_.1, bf16[512,512]{1,0:T(8,128)(2,1)} %refs_1_.1, bf16[8,512]{1,0:T(8,128)(2,1)} %bitcast.6, ...), custom_call_target="tpu_custom_call" | custom-call | tf_op jit(solution)/shard_map/pallas_call | solution.py:785
  153.7 7.9 %shard_map.164 = (bf16[32,8192]{1,0:T(8,128)(2,1)}, bf16[512,512]{1,0:T(8,128)(2,1)}, bf16[512,512]{1,0:T(8,128)(2,1)}, bf16[512,256]{1,0:T(8,128)(2,1)}, bf16[8...) custom-call(bf16[32,8192]{1,0:T(8,128)(2,1)} %get-tuple-element.18.refs_0_, bf16[512,512]{1,0:T(8,128)(2,1)} %get-tuple-element.19.refs_1_, ...), custom_call_target="tpu_custom_call" | custom-call | tf_op jit(solution)/shard_map/pallas_call | solution.py:727

commit v5 on v4

--- a/solution.py
+++ b/solution.py
@@ -654,8 +654,26 @@
     def _():
         give(r.gi).start()
 
-    for number in range(5, 9):
-        gather_matrix.pass_on(number)
+    give(r.gr).wait()
+
+    @pl.when(core == 0)
+    def _():
+        r.g_sum[...] = (r.gi[...] + r.g_there[...]).astype(bf16)
+
+    @pl.when(core == 1)
+    def _():
+        r.g_sum[...] = (r.gr[...] + r.g_there[...]).astype(bf16)
+
+    owner = chip + core * (count // 2)
+
+    @pl.when(owner == place)
+    def _():
+        r.grad_groups[...] = r.g_sum[...]
+
+    @pl.when(owner != place)
+    def _():
+        links.start(r.g_sum, r.grad_groups, {"tensor": owner}).wait()
+
     r.layer_there[place] = r.layer_part[at_rows(place * own_rows, own_rows)]
     for copy in layers_sent:
         copy.wait_recv()
@@ -665,26 +683,8 @@
             total = total + r.layer_there[source].astype(f32)
         r.layer_out[:, half * halfway : (half + 1) * halfway] = total.astype(bf16)
 
-    give(r.gr).wait()
-
-    @pl.when(core == 0)
-    def _():
-        r.g_sum[...] = (r.gi[...] + r.g_there[...]).astype(bf16)
-
-    @pl.when(core == 1)
-    def _():
-        r.g_sum[...] = (r.gr[...] + r.g_there[...]).astype(bf16)
-
-    owner = chip + core * (count // 2)
-
-    @pl.when(owner == place)
-    def _():
-        r.grad_groups[...] = r.g_sum[...]
-
-    @pl.when(owner != place)
-    def _():
-        links.start(r.g_sum, r.grad_groups, {"tensor": owner}).wait()
-
+    for number in range(5, 9):
+        gather_matrix.pass_on(number)
     for copy in stored + [bring_block]:
         copy.wait()
     for copy in parts_sent + layers_sent + [w_sent, squares_sent, normed_sent, within_sent]:

time: 163 us -> 161 us (0.988)
  Pallas kernels: 161 us -> 159 us
    pallas_call x1, Pallas kernels: 153 us -> 151 us  [local(): pl.pallas_call(functools.partial(mixer, names, spread, count), out_shape=...]
where the time goes in v5:
time: 161 us; the launch traced here: 160 us
  Pallas kernels  159 us (99%)
    pallas_call x1, Pallas kernels, local(): pl.pallas_call(functools.partial(mixer, names, spread, count), out_shape=...  151 us
    pallas_call x1, Pallas kernels, hand_over(): pl.pallas_call(body, out_shape=[shape(array.shape, array.dtype) for array...  7.92 us

profile of v5, /device:TPU:11, one launch (start us, length us, event | category | flops | bytes accessed | tf_op | source)
XLA Modules:
  0.0 159.9 jit_solution(6278591331167293907)
XLA Ops:
  0.6 151.2 %shard_map.163 = (bf16[32,8192]{1,0:T(8,128)(2,1)}, bf16[512,512]{1,0:T(8,128)(2,1)}, bf16[512,512]{1,0:T(8,128)(2,1)}, bf16[512,256]{1,0:T(8,128)(2,1)}, bf16[8...) custom-call(bf16[512,512]{1,0:T(8,128)(2,1)} %refs_0_.1, bf16[512,512]{1,0:T(8,128)(2,1)} %refs_1_.1, bf16[8,512]{1,0:T(8,128)(2,1)} %bitcast.6, ...), custom_call_target="tpu_custom_call" | custom-call | tf_op jit(solution)/shard_map/pallas_call | solution.py:785
  151.8 7.9 %shard_map.164 = (bf16[32,8192]{1,0:T(8,128)(2,1)}, bf16[512,512]{1,0:T(8,128)(2,1)}, bf16[512,512]{1,0:T(8,128)(2,1)}, bf16[512,256]{1,0:T(8,128)(2,1)}, bf16[8...) custom-call(bf16[32,8192]{1,0:T(8,128)(2,1)} %get-tuple-element.18.refs_0_, bf16[512,512]{1,0:T(8,128)(2,1)} %get-tuple-element.19.refs_1_, ...), custom_call_target="tpu_custom_call" | custom-call | tf_op jit(solution)/shard_map/pallas_call | solution.py:727
